TPU v7x, 512 devices: a whole 4x4x16 slice. The times are simulated.
512 devices in a mesh: vox: 32 (over z, y_lo), tm: 16 (over y_hi, x, core).
Axes of the slice: x: 4, y: 4 (y_hi: 2, y_lo: 2; y = y_hi * 2 + y_lo), z: 16, core: 2. Of those that a mesh axis runs over, the one named last changes fastest.
Arguments:
- frames_data: bfloat16 [2048, 131072], P('tm', 'vox'), may hold values from -96 to 96
- footprints: bfloat16 [131072, 384], P('vox'), may hold values from 0 to 1, as said below
- traces: bfloat16 [2048, 4096], P('tm', 'vox'), may hold values from 0 to 2
- counts: int32 [32], replicated, may hold values from 1 to 128, 2048 in all
Outputs:
- new_traces: bfloat16 [2048, 4096], P('tm', 'vox')
- products: float32 [131072, 384], P(('vox', 'tm'))
- gram: float32 [12288, 384], P('vox')
Inputs may be any that keep to these rules, and one draw needn't show every extreme that they name: `footprints`: footprint entries are zero or positive. counts of live slots per tile; the largest equals 128.
All inputs are finite; a program needn't handle non-finite values.
Results may differ from a plain program's by a relative error of at most 0.0069.
Values may be sent and summed in bfloat16 or wider, within the bound.
A program may use at most 64 MiB of HBM per device.

v0:
```python
import jax
import jax.numpy as jnp
from jax import lax
from jax.sharding import PartitionSpec as P

ITERS = 4


def padded_2(x, sides, width):
    for axis, dim in sides:
        count, length = (lax.axis_size(axis), x.shape[dim])
        up = [(i, (i + 1) % count) for i in range(count - 1)]
        down = [(j, i) for i, j in up]
        last = lax.slice_in_dim(x, length - width, length, axis=dim)
        first = lax.slice_in_dim(x, 0, width, axis=dim)
        before = lax.ppermute(last, axis, up)
        after = lax.ppermute(first, axis, down)
        x = jnp.concatenate([before, x, after], axis=dim)
    return x


def owner_sums(parts):
    rows, width = parts.shape
    slots = width // 3
    padded = padded_2(parts.reshape(rows, 3, slots), (("vox", 1),), 1)
    return padded[:, 0] + padded[:, 2] + padded[:, 4]


def neighbour_band(current):
    rows, slots = current.shape
    padded = padded_2(current[:, None, :], (("vox", 1),), 1)
    return padded.reshape(rows, 3 * slots)


def frame_product(left, right):
    return lax.dot_general(
        left, right, (((0,), (0,)), ((), ())), preferred_element_type=jnp.float32
    )


def body(frames_data, footprints, traces, counts):
    slots = traces.shape[1]
    tiles = counts.shape[0]
    tile = lax.axis_index("vox")
    wanted = tile + jnp.arange(3, dtype=jnp.int32) - 1
    match = wanted[:, None] == jnp.arange(tiles, dtype=jnp.int32)[None, :]
    number = jnp.sum(jnp.where(match, counts[None, :], 0), axis=1)
    live = (jnp.arange(slots, dtype=jnp.int32)[None, :] < number[:, None]).reshape(3 * slots)
    blocks = footprints * live[None, :].astype(footprints.dtype)
    own_live = live[slots : 2 * slots].astype(jnp.float32)
    current = traces * own_live.astype(traces.dtype)[None, :]
    support = jnp.sum(blocks.astype(jnp.float32), axis=1).astype(jnp.bfloat16)
    reach = jnp.dot(support[None, :], blocks, preferred_element_type=jnp.float32)
    majorant = jnp.maximum(owner_sums(reach)[0], 1.0)
    for step in range(ITERS):
        band = neighbour_band(current)
        recon = lax.dot_general(
            band, blocks, (((1,), (1,)), ((), ())), preferred_element_type=jnp.float32
        )
        resid = (frames_data.astype(jnp.float32) - recon).astype(jnp.bfloat16)
        slope = owner_sums(jnp.dot(resid, blocks, preferred_element_type=jnp.float32))
        updated = jnp.maximum(current.astype(jnp.float32) + slope / majorant[None, :], 0.0)
        current = (updated * own_live[None, :]).astype(jnp.bfloat16)
    band = neighbour_band(current)
    share_rows = frames_data.shape[1] // lax.axis_size("tm")
    full = frame_product(frames_data, band)
    gram_part = frame_product(band, band)
    total, gram = lax.psum((full, gram_part), "tm")
    products = lax.dynamic_slice_in_dim(total, lax.axis_index("tm") * share_rows, share_rows, 0)
    return (current, products, gram)


def solution(mesh):
    return jax.shard_map(
        body,
        mesh=mesh,
        in_specs=(P("tm", "vox"), P("vox", None), P("tm", "vox"), P()),
        out_specs=(P("tm", "vox"), P(("vox", "tm"), None), P("vox", None)),
        check_vma=False,
    )
```

profile of v0, /device:TPU:1, one launch (start us, length us, event | category | flops | bytes accessed | tf_op | source)
XLA Modules:
  0.0 336.4 jit_solution(15355210743176837951)
XLA Ops:
  7.2 0.0 all-reduce.3.cloned.1.call-start
  7.2 0.8 select_reduce_fusion
  8.1 0.1 iota_compare_fusion.1
  8.2 0.9 copy.28
  9.0 0.1 multiply_bitcast_fusion
  9.1 1.3 collective-permute-start.1
  10.4 4.7 %collective-permute-start = (bf16[128,1,128]{0,2,1:T(8,128)(2,1)S(1)}, bf16[128,1,128]{0,2,1:T(8,128)(2,1)S(1)}, u32[]{:S(2)}, u32[]{:S(2)}) collective-permute-start(bf16[128,1,128]{0,2,1:T(8,128)(2,1)S(1)} %multiply_bitcast_fusion), channel_id=1, source_target_pairs={{0,16},{16,32},{32,48},{48,64},{64,80},{80,96},{96,112},{112,128},... | collective-permute-start | bytes 98312 | tf_op jit(solution)/shard_map/ppermute | solution.py:16
  15.1 4.8 %copy.29 = bf16[4096,384]{0,1:T(8,128)(2,1)} copy(bf16[4096,384]{1,0:T(8,128)(2,1)} %param.5) | data formatting | bytes 6291456 | tf_op args[1]
  19.8 3.1 fusion.39
  22.9 0.9 fusion.44
  23.9 4.3 %collective-permute-start.4 = (f32[1,1,128]{2,1,0:T(1,128)S(1)}, f32[1,1,128]{2,1,0:T(1,128)S(1)}, u32[]{:S(2)}, u32[]{:S(2)}) collective-permute-start(f32[1,1,128]{2,1,0:T(1,128)S(1)} %get-tuple-element.24), channel_id=1, source_target_pairs={{0,16},{16,32},{32,48},{48,64},{64,80},{80,96},{96,112},{112,128},... | collective-permute-start | bytes 1544 | tf_op jit(solution)/shard_map/ppermute | solution.py:16
  28.1 1.3 collective-permute-start.5
  29.4 0.0 collective-permute-done.1
  29.4 0.0 collective-permute-done
  29.5 2.8 fusion.7
  32.3 4.0 %collective-permute-start.2 = (f32[128,1,128]{0,2,1:T(8,128)S(1)}, f32[128,1,128]{0,2,1:T(8,128)S(1)}, u32[]{:S(2)}, u32[]{:S(2)}) collective-permute-start(f32[128,1,128]{0,2,1:T(8,128)S(1)} %get-tuple-element.22), channel_id=1, source_target_pairs={{0,16},{16,32},{32,48},{48,64},{64,80},{80,96},{96,112},{112,128},... | collective-permute-start | bytes 196616 | tf_op jit(solution)/shard_map/ppermute | solution.py:16
  36.3 1.3 collective-permute-start.3
  37.6 0.0 collective-permute-done.4
  37.6 0.0 collective-permute-done.5
  37.6 0.0 collective-permute-done.2
  37.6 3.7 %collective-permute-done.3 = f32[128,1,128]{0,2,1:T(8,128)S(1)} collective-permute-done((f32[128,1,128]{0,2,1:T(8,128)S(1)}, f32[128,1,128]{0,2,1:T(8,128)S(1)}, u32[]{:S(2)}, u32[]{:S(2)}) %collective-permute-start.3) | collective-permute-done | bytes 65568 | tf_op jit(solution)/shard_map/ppermute | solution.py:17
  41.4 0.1 fusion.32
  41.5 1.3 collective-permute-start.7
  42.8 4.9 %collective-permute-start.6 = (bf16[128,1,128]{0,2,1:T(8,128)(2,1)S(1)}, bf16[128,1,128]{0,2,1:T(8,128)(2,1)S(1)}, u32[]{:S(2)}, u32[]{:S(2)}) collective-permute-start(bf16[128,1,128]{0,2,1:T(8,128)(2,1)S(1)} %bitcast.129), channel_id=1, source_target_pairs={{0,16},{16,32},{32,48},{48,64},{64,80},{80,96},{96,112},{112,128},... | collective-permute-start | bytes 98312 | tf_op jit(solution)/shard_map/ppermute | solution.py:16
  47.7 0.0 collective-permute-done.7
  47.7 1.0 collective-permute-done.6
  48.7 2.8 fusion.6
  51.5 4.3 %collective-permute-start.8 = (f32[128,1,128]{0,2,1:T(8,128)S(1)}, f32[128,1,128]{0,2,1:T(8,128)S(1)}, u32[]{:S(2)}, u32[]{:S(2)}) collective-permute-start(f32[128,1,128]{0,2,1:T(8,128)S(1)} %get-tuple-element.20), channel_id=1, source_target_pairs={{0,16},{16,32},{32,48},{48,64},{64,80},{80,96},{96,112},{112,128},... | collective-permute-start | bytes 196616 | tf_op jit(solution)/shard_map/ppermute | solution.py:16
  55.8 1.3 collective-permute-start.9
  57.1 0.0 collective-permute-done.8
  57.1 5.0 %collective-permute-done.9 = f32[128,1,128]{0,2,1:T(8,128)S(1)} collective-permute-done((f32[128,1,128]{0,2,1:T(8,128)S(1)}, f32[128,1,128]{0,2,1:T(8,128)S(1)}, u32[]{:S(2)}, u32[]{:S(2)}) %collective-permute-start.9) | collective-permute-done | bytes 65568 | tf_op jit(solution)/shard_map/ppermute | solution.py:17
  62.1 0.1 fusion.33
  62.2 1.3 collective-permute-start.11
  63.5 4.9 %collective-permute-start.10 = (bf16[128,1,128]{0,2,1:T(8,128)(2,1)S(1)}, bf16[128,1,128]{0,2,1:T(8,128)(2,1)S(1)}, u32[]{:S(2)}, u32[]{:S(2)}) collective-permute-start(bf16[128,1,128]{0,2,1:T(8,128)(2,1)S(1)} %bitcast.132), channel_id=1, source_target_pairs={{0,16},{16,32},{32,48},{48,64},{64,80},{80,96},{96,112},{112,128},... | collective-permute-start | bytes 98312 | tf_op jit(solution)/shard_map/ppermute | solution.py:16
  68.4 0.0 collective-permute-done.11
  68.4 1.0 collective-permute-done.10
  69.4 2.8 fusion.5
  72.2 4.3 %collective-permute-start.12 = (f32[128,1,128]{0,2,1:T(8,128)S(1)}, f32[128,1,128]{0,2,1:T(8,128)S(1)}, u32[]{:S(2)}, u32[]{:S(2)}) collective-permute-start(f32[128,1,128]{0,2,1:T(8,128)S(1)} %get-tuple-element.18), channel_id=1, source_target_pairs={{0,16},{16,32},{32,48},{48,64},{64,80},{80,96},{96,112},{112,128},... | collective-permute-start | bytes 196616 | tf_op jit(solution)/shard_map/ppermute | solution.py:16
  76.5 1.3 collective-permute-start.13
  77.8 0.2 collective-permute-done.12
  78.0 4.7 %collective-permute-done.13 = f32[128,1,128]{0,2,1:T(8,128)S(1)} collective-permute-done((f32[128,1,128]{0,2,1:T(8,128)S(1)}, f32[128,1,128]{0,2,1:T(8,128)S(1)}, u32[]{:S(2)}, u32[]{:S(2)}) %collective-permute-start.13) | collective-permute-done | bytes 65568 | tf_op jit(solution)/shard_map/ppermute | solution.py:17
  82.7 0.1 fusion.34
  82.8 1.3 collective-permute-start.15
  84.1 4.9 %collective-permute-start.14 = (bf16[128,1,128]{0,2,1:T(8,128)(2,1)S(1)}, bf16[128,1,128]{0,2,1:T(8,128)(2,1)S(1)}, u32[]{:S(2)}, u32[]{:S(2)}) collective-permute-start(bf16[128,1,128]{0,2,1:T(8,128)(2,1)S(1)} %bitcast.126), channel_id=1, source_target_pairs={{0,16},{16,32},{32,48},{48,64},{64,80},{80,96},{96,112},{112,128},... | collective-permute-start | bytes 98312 | tf_op jit(solution)/shard_map/ppermute | solution.py:16
  89.0 0.0 collective-permute-done.15
  89.0 1.0 collective-permute-done.14
  90.0 2.8 fusion.4
  92.8 4.3 %collective-permute-start.16 = (f32[128,1,128]{0,2,1:T(8,128)S(1)}, f32[128,1,128]{0,2,1:T(8,128)S(1)}, u32[]{:S(2)}, u32[]{:S(2)}) collective-permute-start(f32[128,1,128]{0,2,1:T(8,128)S(1)} %get-tuple-element.16), channel_id=1, source_target_pairs={{0,16},{16,32},{32,48},{48,64},{64,80},{80,96},{96,112},{112,128},... | collective-permute-start | bytes 196616 | tf_op jit(solution)/shard_map/ppermute | solution.py:16
  97.1 1.3 collective-permute-start.17
  98.4 0.0 collective-permute-done.16
  98.4 4.9 %collective-permute-done.17 = f32[128,1,128]{0,2,1:T(8,128)S(1)} collective-permute-done((f32[128,1,128]{0,2,1:T(8,128)S(1)}, f32[128,1,128]{0,2,1:T(8,128)S(1)}, u32[]{:S(2)}, u32[]{:S(2)}) %collective-permute-start.17) | collective-permute-done | bytes 65568 | tf_op jit(solution)/shard_map/ppermute | solution.py:17
  103.3 0.1 fusion.35
  103.4 1.3 collective-permute-start.19
  104.7 6.1 %collective-permute-start.18 = (bf16[128,1,128]{0,2,1:T(8,128)(2,1)S(1)}, bf16[128,1,128]{0,2,1:T(8,128)(2,1)S(1)}, u32[]{:S(2)}, u32[]{:S(2)}) collective-permute-start(bf16[128,1,128]{0,2,1:T(8,128)(2,1)S(1)} %bitcast.123), channel_id=1, source_target_pairs={{0,16},{16,32},{32,48},{48,64},{64,80},{80,96},{96,112},{112,128},... | collective-permute-start | bytes 98312 | tf_op jit(solution)/shard_map/ppermute | solution.py:16
  110.8 0.0 collective-permute-done.19
  110.9 1.2 collective-permute-done.18
  112.0 1.1 fusion.45
  113.1 4.8 %convolution_bitcast_fusion = f32[4096,384]{0,1:T(8,128)} fusion(bf16[128,384]{0,1:T(8,128)(2,1)S(1)} %bitcast.109, bf16[128,4096]{1,0:T(8,128)(2,1)} %param.4), kind=kOutput, calls=%fused_computation | convolution fusion | flops 402653184 | bytes 7438336 | tf_op jit(solution)/shard_map/dot_general | solution.py:36
  117.9 0.0 all-reduce.3.cloned.1.call-update
  117.9 0.7 copy.34
  118.7 207.0 %all-reduce.3.cloned.1.call-done = (f32[4096,384]{0,1:T(8,128)}, f32[384,384]{1,0:T(8,128)}) async-done(((f32[4096,384]{0,1:T(8,128)}, f32[384,384]{1,0:T(8,128)}), (f32[4096,384]{0,1:T(8,128)}, f32[384,384]{1,0:T(8,128)})) %all-reduce.3.cloned.1.call-update) | async-done | bytes 6881296 | tf_op jit(solution)/shard_map/psum | solution.py:68
  325.7 1.0 constant_dynamic-slice_fusion
  326.7 0.9 copy.35
  327.6 1.9 copy.46
  (14 shorter events, 0.2 us)
Async XLA Ops:
  7.2 318.5 %all-reduce.3.cloned.1.call-start = ((), (), s32[]{:S(2)}) async-start(), calls=%async_computation | async-start | bytes 13762560 | tf_op jit(solution)/shard_map/psum | solution.py:68
  9.1 20.3 %collective-permute-start.1 = (bf16[128,1,128]{0,2,1:T(8,128)(2,1)S(1)}, bf16[128,1,128]{0,2,1:T(8,128)(2,1)S(1)}, u32[]{:S(2)}, u32[]{:S(2)}) collective-permute-start(bf16[128,1,128]{0,2,1:T(8,128)(2,1)S(1)} %multiply_bitcast_fusion), channel_id=1, source_target_pairs={{16,0},{32,16},{48,32},{64,48},{80,64},{96,80},{112,96},{128,112},... | collective-permute-start | bytes 98312 | tf_op jit(solution)/shard_map/ppermute | solution.py:17
  10.4 19.0 %collective-permute-start = (bf16[128,1,128]{0,2,1:T(8,128)(2,1)S(1)}, bf16[128,1,128]{0,2,1:T(8,128)(2,1)S(1)}, u32[]{:S(2)}, u32[]{:S(2)}) collective-permute-start(bf16[128,1,128]{0,2,1:T(8,128)(2,1)S(1)} %multiply_bitcast_fusion), channel_id=1, source_target_pairs={{0,16},{16,32},{32,48},{48,64},{64,80},{80,96},{96,112},{112,128},... | collective-permute-start | bytes 98312 | tf_op jit(solution)/shard_map/ppermute | solution.py:16
  23.9 13.7 %collective-permute-start.4 = (f32[1,1,128]{2,1,0:T(1,128)S(1)}, f32[1,1,128]{2,1,0:T(1,128)S(1)}, u32[]{:S(2)}, u32[]{:S(2)}) collective-permute-start(f32[1,1,128]{2,1,0:T(1,128)S(1)} %get-tuple-element.24), channel_id=1, source_target_pairs={{0,16},{16,32},{32,48},{48,64},{64,80},{80,96},{96,112},{112,128},... | collective-permute-start | bytes 1544 | tf_op jit(solution)/shard_map/ppermute | solution.py:16
  28.1 9.5 %collective-permute-start.5 = (f32[1,1,128]{2,1,0:T(1,128)S(1)}, f32[1,1,128]{2,1,0:T(1,128)S(1)}, u32[]{:S(2)}, u32[]{:S(2)}) collective-permute-start(f32[1,1,128]{2,1,0:T(1,128)S(1)} %get-tuple-element.25), channel_id=1, source_target_pairs={{16,0},{32,16},{48,32},{64,48},{80,64},{96,80},{112,96},{128,112},... | collective-permute-start | bytes 1544 | tf_op jit(solution)/shard_map/ppermute | solution.py:17
  32.3 5.3 %collective-permute-start.2 = (f32[128,1,128]{0,2,1:T(8,128)S(1)}, f32[128,1,128]{0,2,1:T(8,128)S(1)}, u32[]{:S(2)}, u32[]{:S(2)}) collective-permute-start(f32[128,1,128]{0,2,1:T(8,128)S(1)} %get-tuple-element.22), channel_id=1, source_target_pairs={{0,16},{16,32},{32,48},{48,64},{64,80},{80,96},{96,112},{112,128},... | collective-permute-start | bytes 196616 | tf_op jit(solution)/shard_map/ppermute | solution.py:16
  36.3 5.1 %collective-permute-start.3 = (f32[128,1,128]{0,2,1:T(8,128)S(1)}, f32[128,1,128]{0,2,1:T(8,128)S(1)}, u32[]{:S(2)}, u32[]{:S(2)}) collective-permute-start(f32[128,1,128]{0,2,1:T(8,128)S(1)} %get-tuple-element.23), channel_id=1, source_target_pairs={{16,0},{32,16},{48,32},{64,48},{80,64},{96,80},{112,96},{128,112},... | collective-permute-start | bytes 196616 | tf_op jit(solution)/shard_map/ppermute | solution.py:17
  41.5 6.2 %collective-permute-start.7 = (bf16[128,1,128]{0,2,1:T(8,128)(2,1)S(1)}, bf16[128,1,128]{0,2,1:T(8,128)(2,1)S(1)}, u32[]{:S(2)}, u32[]{:S(2)}) collective-permute-start(bf16[128,1,128]{0,2,1:T(8,128)(2,1)S(1)} %bitcast.128), channel_id=1, source_target_pairs={{16,0},{32,16},{48,32},{64,48},{80,64},{96,80},{112,96},{128,112},... | collective-permute-start | bytes 98312 | tf_op jit(solution)/shard_map/ppermute | solution.py:17
  42.8 5.9 %collective-permute-start.6 = (bf16[128,1,128]{0,2,1:T(8,128)(2,1)S(1)}, bf16[128,1,128]{0,2,1:T(8,128)(2,1)S(1)}, u32[]{:S(2)}, u32[]{:S(2)}) collective-permute-start(bf16[128,1,128]{0,2,1:T(8,128)(2,1)S(1)} %bitcast.129), channel_id=1, source_target_pairs={{0,16},{16,32},{32,48},{48,64},{64,80},{80,96},{96,112},{112,128},... | collective-permute-start | bytes 98312 | tf_op jit(solution)/shard_map/ppermute | solution.py:16
  51.5 5.6 %collective-permute-start.8 = (f32[128,1,128]{0,2,1:T(8,128)S(1)}, f32[128,1,128]{0,2,1:T(8,128)S(1)}, u32[]{:S(2)}, u32[]{:S(2)}) collective-permute-start(f32[128,1,128]{0,2,1:T(8,128)S(1)} %get-tuple-element.20), channel_id=1, source_target_pairs={{0,16},{16,32},{32,48},{48,64},{64,80},{80,96},{96,112},{112,128},... | collective-permute-start | bytes 196616 | tf_op jit(solution)/shard_map/ppermute | solution.py:16
  55.8 6.3 %collective-permute-start.9 = (f32[128,1,128]{0,2,1:T(8,128)S(1)}, f32[128,1,128]{0,2,1:T(8,128)S(1)}, u32[]{:S(2)}, u32[]{:S(2)}) collective-permute-start(f32[128,1,128]{0,2,1:T(8,128)S(1)} %get-tuple-element.21), channel_id=1, source_target_pairs={{16,0},{32,16},{48,32},{64,48},{80,64},{96,80},{112,96},{128,112},... | collective-permute-start | bytes 196616 | tf_op jit(solution)/shard_map/ppermute | solution.py:17
  62.2 6.2 %collective-permute-start.11 = (bf16[128,1,128]{0,2,1:T(8,128)(2,1)S(1)}, bf16[128,1,128]{0,2,1:T(8,128)(2,1)S(1)}, u32[]{:S(2)}, u32[]{:S(2)}) collective-permute-start(bf16[128,1,128]{0,2,1:T(8,128)(2,1)S(1)} %bitcast.131), channel_id=1, source_target_pairs={{16,0},{32,16},{48,32},{64,48},{80,64},{96,80},{112,96},{128,112},... | collective-permute-start | bytes 98312 | tf_op jit(solution)/shard_map/ppermute | solution.py:17
  63.5 5.9 %collective-permute-start.10 = (bf16[128,1,128]{0,2,1:T(8,128)(2,1)S(1)}, bf16[128,1,128]{0,2,1:T(8,128)(2,1)S(1)}, u32[]{:S(2)}, u32[]{:S(2)}) collective-permute-start(bf16[128,1,128]{0,2,1:T(8,128)(2,1)S(1)} %bitcast.132), channel_id=1, source_target_pairs={{0,16},{16,32},{32,48},{48,64},{64,80},{80,96},{96,112},{112,128},... | collective-permute-start | bytes 98312 | tf_op jit(solution)/shard_map/ppermute | solution.py:16
  72.2 5.8 %collective-permute-start.12 = (f32[128,1,128]{0,2,1:T(8,128)S(1)}, f32[128,1,128]{0,2,1:T(8,128)S(1)}, u32[]{:S(2)}, u32[]{:S(2)}) collective-permute-start(f32[128,1,128]{0,2,1:T(8,128)S(1)} %get-tuple-element.18), channel_id=1, source_target_pairs={{0,16},{16,32},{32,48},{48,64},{64,80},{80,96},{96,112},{112,128},... | collective-permute-start | bytes 196616 | tf_op jit(solution)/shard_map/ppermute | solution.py:16
  76.5 6.2 %collective-permute-start.13 = (f32[128,1,128]{0,2,1:T(8,128)S(1)}, f32[128,1,128]{0,2,1:T(8,128)S(1)}, u32[]{:S(2)}, u32[]{:S(2)}) collective-permute-start(f32[128,1,128]{0,2,1:T(8,128)S(1)} %get-tuple-element.19), channel_id=1, source_target_pairs={{16,0},{32,16},{48,32},{64,48},{80,64},{96,80},{112,96},{128,112},... | collective-permute-start | bytes 196616 | tf_op jit(solution)/shard_map/ppermute | solution.py:17
  82.8 6.2 %collective-permute-start.15 = (bf16[128,1,128]{0,2,1:T(8,128)(2,1)S(1)}, bf16[128,1,128]{0,2,1:T(8,128)(2,1)S(1)}, u32[]{:S(2)}, u32[]{:S(2)}) collective-permute-start(bf16[128,1,128]{0,2,1:T(8,128)(2,1)S(1)} %bitcast.125), channel_id=1, source_target_pairs={{16,0},{32,16},{48,32},{64,48},{80,64},{96,80},{112,96},{128,112},... | collective-permute-start | bytes 98312 | tf_op jit(solution)/shard_map/ppermute | solution.py:17
  84.1 5.9 %collective-permute-start.14 = (bf16[128,1,128]{0,2,1:T(8,128)(2,1)S(1)}, bf16[128,1,128]{0,2,1:T(8,128)(2,1)S(1)}, u32[]{:S(2)}, u32[]{:S(2)}) collective-permute-start(bf16[128,1,128]{0,2,1:T(8,128)(2,1)S(1)} %bitcast.126), channel_id=1, source_target_pairs={{0,16},{16,32},{32,48},{48,64},{64,80},{80,96},{96,112},{112,128},... | collective-permute-start | bytes 98312 | tf_op jit(solution)/shard_map/ppermute | solution.py:16
  92.8 5.6 %collective-permute-start.16 = (f32[128,1,128]{0,2,1:T(8,128)S(1)}, f32[128,1,128]{0,2,1:T(8,128)S(1)}, u32[]{:S(2)}, u32[]{:S(2)}) collective-permute-start(f32[128,1,128]{0,2,1:T(8,128)S(1)} %get-tuple-element.16), channel_id=1, source_target_pairs={{0,16},{16,32},{32,48},{48,64},{64,80},{80,96},{96,112},{112,128},... | collective-permute-start | bytes 196616 | tf_op jit(solution)/shard_map/ppermute | solution.py:16
  97.1 6.2 %collective-permute-start.17 = (f32[128,1,128]{0,2,1:T(8,128)S(1)}, f32[128,1,128]{0,2,1:T(8,128)S(1)}, u32[]{:S(2)}, u32[]{:S(2)}) collective-permute-start(f32[128,1,128]{0,2,1:T(8,128)S(1)} %get-tuple-element.17), channel_id=1, source_target_pairs={{16,0},{32,16},{48,32},{64,48},{80,64},{96,80},{112,96},{128,112},... | collective-permute-start | bytes 196616 | tf_op jit(solution)/shard_map/ppermute | solution.py:17
  103.4 7.4 %collective-permute-start.19 = (bf16[128,1,128]{0,2,1:T(8,128)(2,1)S(1)}, bf16[128,1,128]{0,2,1:T(8,128)(2,1)S(1)}, u32[]{:S(2)}, u32[]{:S(2)}) collective-permute-start(bf16[128,1,128]{0,2,1:T(8,128)(2,1)S(1)} %bitcast.122), channel_id=1, source_target_pairs={{16,0},{32,16},{48,32},{64,48},{80,64},{96,80},{112,96},{128,112},... | collective-permute-start | bytes 98312 | tf_op jit(solution)/shard_map/ppermute | solution.py:17
  104.7 7.3 %collective-permute-start.18 = (bf16[128,1,128]{0,2,1:T(8,128)(2,1)S(1)}, bf16[128,1,128]{0,2,1:T(8,128)(2,1)S(1)}, u32[]{:S(2)}, u32[]{:S(2)}) collective-permute-start(bf16[128,1,128]{0,2,1:T(8,128)(2,1)S(1)} %bitcast.123), channel_id=1, source_target_pairs={{0,16},{16,32},{32,48},{48,64},{64,80},{80,96},{96,112},{112,128},... | collective-permute-start | bytes 98312 | tf_op jit(solution)/shard_map/ppermute | solution.py:16
Sparse Core Ops, SparseCore 0:
  118.1 207.6 all-reduce.2
where the time goes:
time: 338 us; the launch traced here: 336 us
  waiting for transfers between devices  230 us (68%)
  starting transfers between devices  59.4 us (18%)
  matrix products  18 us (5%)
  between operations  14.4 us (4%)
  local copies, waits for them, and re-layouts  10.3 us (3%)
  other arithmetic  4.59 us (1%)
    psum x1, waiting for transfers between devices, body(): total, gram = lax.psum((full, gram_part), 'tm')  207 us
    ppermute x10, starting transfers between devices, padded_2(): before = lax.ppermute(last, axis, up)  46.5 us
    ppermute x10, waiting for transfers between devices, padded_2(): after = lax.ppermute(first, axis, down)  18.3 us
    ppermute x10, starting transfers between devices, padded_2(): after = lax.ppermute(first, axis, down)  12.9 us
    dot_general x4, matrix products, body(): jnp.dot(resid, blocks, preferred_element_type=jnp.float32)  11.2 us
    unnamed x6, local copies, waits for them, and re-layouts  9.18 us
  transfers between devices with their start and end apart: 21, of which 10 were waited for; matrix products, arithmetic and copies ran while one was open for 4% of the time, Pallas kernels for 0%

commit v1 on v0

v1 whole, which is shorter than its diff:
```python
import functools

import jax
import jax.numpy as jnp
from jax import lax
from jax.experimental import pallas as pl
from jax.experimental.pallas import tpu as pltpu
from jax.sharding import PartitionSpec as P

ITERS = 4
CHUNK = 512
MESH = pl.DeviceIdType.MESH
F32 = jnp.float32
BF16 = jnp.bfloat16


def position():
    vox, tm = lax.axis_index("vox"), lax.axis_index("tm")
    return vox // 2, vox % 2, tm // 2, tm % 2


def turned(quad, dy, dx):
    return ((quad // 4 + dy) % 2) * 4 + (quad % 4 + dx) % 4


def exchange_kernel(
    planes,
    counts_ref, frames_ref, prints_ref, traces_ref,
    movie_ref, band_ref, edge_ref,
    prints, frames, tracebuf, gacc, facc,
    part_plane, part_edge, got_plane, got_edge,
    gram_plane, gram_edge, got_gram, mixing,
    state, final, final_edge,
    load_sem, movie_send, movie_recv, trace_send, trace_recv, part_send, part_recv,
    gram_send, gram_recv, state_send, state_recv, band_send, band_recv,
    edge_send, edge_recv, pass_send, pass_recv, own_sem,
):
    z, l, quad, core = position()
    other = 1 - l
    up, down = (z + 1) % planes, (z + planes - 1) % planes
    outward = (z + planes - 1 + 2 * l) % planes

    def device(plane, side, q, c):
        return (plane * 2 + side, q * 2 + c)

    me = device(z, l, quad, core)
    offsets = [(dy, dx) for dy in range(2) for dx in range(4)]
    barrier = pltpu.get_barrier_semaphore()
    greeted = 0
    for dy, dx in offsets:
        back = turned(quad, -dy + 2, -dx + 4)
        for dc in range(2):
            if (dy, dx, dc) != (0, 0, 0):
                pl.semaphore_signal(barrier, inc=1, device_id=device(z, l, back, (core + dc) % 2), device_id_type=MESH)
                greeted += 1
        pl.semaphore_signal(barrier, inc=1, device_id=device(z, other, back, core), device_id_type=MESH)
        greeted += 1
        inward = (z + planes + 2 * l - 1) % planes
        for side in range(2):
            pl.semaphore_signal(barrier, inc=1, device_id=device(inward, side, back, core), device_id_type=MESH)
            greeted += 1
    far = (z + planes + 1 - 2 * l) % planes
    for side in range(2):
        pl.semaphore_signal(barrier, inc=1, device_id=device(far, side, quad, core), device_id_type=MESH)
        greeted += 1

    rows = prints_ref.shape[0]
    chunks = rows // CHUNK
    plane_at = pl.multiple_of((1 - l) * 128, 128)
    edge_at = pl.multiple_of(l * 256, 128)

    def loads(k):
        at = pl.multiple_of(k * CHUNK, CHUNK)
        return (
            pltpu.make_async_copy(prints_ref.at[pl.ds(at, CHUNK), pl.ds(plane_at, 256)], prints.at[pl.ds(at, CHUNK), pl.ds(0, 256)], load_sem.at[k, 0]),
            pltpu.make_async_copy(prints_ref.at[pl.ds(at, CHUNK), pl.ds(edge_at, 128)], prints.at[pl.ds(at, CHUNK), pl.ds(256, 128)], load_sem.at[k, 1]),
            pltpu.make_async_copy(frames_ref.at[:, :, pl.ds(at, CHUNK)], frames.at[:, :, pl.ds(at, CHUNK)], load_sem.at[k, 2]),
        )

    own_trace = pltpu.make_async_copy(traces_ref, tracebuf.at[2 + l], own_sem.at[0])
    own_trace.start()
    for k in range(chunks):
        for copy in loads(k):
            copy.start()
    share = movie_ref.shape[4]
    own_movie = pltpu.make_async_copy(
        frames_ref.at[:, :, pl.ds(pl.multiple_of((quad * 2 + core) * share, share), share)],
        movie_ref.at[core, :, quad], own_sem.at[1])
    own_movie.start()

    pl.semaphore_wait(barrier, greeted)

    def trace_copy(k, plane, side, slot):
        return pltpu.make_async_remote_copy(
            traces_ref, tracebuf.at[slot], trace_send.at[k], trace_recv.at[slot],
            device_id=device(plane, side, quad, core), device_id_type=MESH)

    trace_copies = [
        trace_copy(0, z, other, 2 + l),
        trace_copy(1, up, 0, l), trace_copy(2, up, 1, l),
        trace_copy(3, down, 0, 4 + l), trace_copy(4, down, 1, 4 + l),
    ]
    for copy in trace_copies:
        copy.start()

    movie_copies = []
    for dc in range(2):
        for dy, dx in offsets:
            if (dy, dx, dc) != (0, 0, 0):
                q, c = turned(quad, dy, dx), (core + dc) % 2
                slot = (dy * 4 + dx) * 2 + dc
                movie_copies.append(pltpu.make_async_remote_copy(
                    frames_ref.at[:, :, pl.ds(pl.multiple_of((q * 2 + c) * share, share), share)],
                    movie_ref.at[core, :, quad], movie_send.at[slot], movie_recv.at[slot],
                    device_id=device(z, l, q, c), device_id_type=MESH))
    for copy in movie_copies:
        copy.start()

    def number(tile):
        inside = jnp.logical_and(tile >= 0, tile < 2 * planes)
        return jnp.where(inside, counts_ref[jnp.clip(tile, 0, 2 * planes - 1)], 0)

    numbers = [number(2 * z - 2 + s) for s in range(6)]
    edge_number = jnp.where(l == 0, numbers[1], numbers[4])

    lane = lax.broadcasted_iota(jnp.int32, (1, 128), 1)
    row = lax.broadcasted_iota(jnp.int32, (128, 1), 0)
    live_rows = jnp.concatenate(
        [(row < n).astype(F32) for n in (numbers[2], numbers[3], edge_number)], axis=0)
    live_lanes = [(lane < n).astype(F32) for n in numbers]
    own_live = jnp.concatenate([live_lanes[2], live_lanes[3]], axis=1)

    gacc[...] = jnp.zeros_like(gacc)
    facc[...] = jnp.zeros_like(facc)

    def chunk_step(k, carry):
        for copy in loads(k):
            copy.wait()
        at = pl.multiple_of(k * CHUNK, CHUNK)
        block = prints[pl.ds(at, CHUNK), :]
        turned_block = block.T
        support = jnp.sum(turned_block.astype(F32) * live_rows, axis=0, keepdims=True).astype(BF16)
        left = jnp.concatenate(
            [frames[0, :, pl.ds(at, CHUNK)], frames[1, :, pl.ds(at, CHUNK)],
             jnp.broadcast_to(support, (16, CHUNK))], axis=0)
        facc[...] += jnp.dot(left, block, preferred_element_type=F32)
        gacc[...] += jnp.dot(turned_block, block, preferred_element_type=F32)
        return carry

    lax.fori_loop(0, chunks, chunk_step, 0)

    gram = gacc[...]
    high = gram.astype(BF16)
    low = (gram - high.astype(F32)).astype(BF16)
    gram_plane[l] = high[:, :256]
    gram_edge[...] = high[:, 256:]

    own_trace.wait()

    def trace_arrival(slot):
        pltpu.make_async_remote_copy(
            traces_ref, tracebuf.at[slot], trace_send.at[0], trace_recv.at[slot],
            device_id=me, device_id_type=MESH).wait_recv()

    for slot in (0, 1, 4, 5):
        trace_arrival(slot)
    trace_arrival(2 + other)

    def trace(slot, live):
        return (tracebuf[slot].astype(F32) * live).astype(BF16)

    edge_live = jnp.where(l == 0, live_lanes[1], live_lanes[4])
    band = jnp.concatenate(
        [trace(2, live_lanes[2]), trace(3, live_lanes[3]), trace(1 + 3 * l, edge_live)], axis=1)
    reach = facc[128:136, :]
    parts = facc[0:128, :] - jnp.dot(band, high, preferred_element_type=F32) - jnp.dot(band, low, preferred_element_type=F32)
    for half in range(2):
        piece = jnp.concatenate([parts[half * 64:half * 64 + 64], reach], axis=0)
        part_plane[half] = piece[:, :256]
        part_edge[half] = piece[:, 256:]

    def to(src, dst, send, recv, plane, side):
        return pltpu.make_async_remote_copy(
            src, dst, send, recv, device_id=device(plane, side, quad, core), device_id_type=MESH)

    part_copies = [
        to(part_plane.at[other], got_plane, part_send.at[0], part_recv.at[2], z, other),
        to(part_edge.at[l], got_edge.at[other], part_send.at[1], part_recv.at[other], outward, l),
        to(part_edge.at[other], got_edge.at[other], part_send.at[2], part_recv.at[other], outward, other),
    ]
    gram_copies = [
        to(gram_plane.at[l], gram_plane.at[l], gram_send.at[0], gram_recv.at[2], z, other),
        to(gram_edge, got_gram.at[other], gram_send.at[1], gram_recv.at[other], outward, l),
        to(gram_edge, got_gram.at[other], gram_send.at[2], gram_recv.at[other], outward, other),
    ]
    for copy in part_copies + gram_copies:
        copy.start()

    mine = pl.ds(pl.multiple_of(l * 64, 64), 64)
    for s in range(6):
        value = (tracebuf[s, mine, :].astype(F32) * live_lanes[s]).astype(BF16)
        state[0, s // 2, :, (s % 2) * 128:(s % 2) * 128 + 128] = value

    to(part_plane.at[0], got_plane, part_send.at[0], part_recv.at[2], z, other).wait_recv()
    for slot in range(2):
        to(part_edge.at[0], got_edge.at[slot], part_send.at[0], part_recv.at[slot], z, other).wait_recv()
    below, above = z > 0, z < planes - 1
    total = part_plane[l] + got_plane[...] + jnp.concatenate(
        [jnp.where(below, got_edge[0], 0.0), jnp.where(above, got_edge[1], 0.0)], axis=1)
    slope = total[0:64]
    majorant = jnp.maximum(total[64:65], 1.0)

    def updated(current, slope):
        value = jnp.maximum(current.astype(F32) + slope / majorant, 0.0)
        return (value * own_live).astype(BF16)

    def send_state(step):
        copies = [
            to(state.at[step, 1], state.at[step, 0], state_send.at[step, 0], state_recv.at[step, 0], up, l),
            to(state.at[step, 1], state.at[step, 2], state_send.at[step, 1], state_recv.at[step, 1], down, l),
        ]
        for copy in copies:
            copy.start()
        return copies

    def full_state(step):
        left = jnp.where(below, state[step, 0], jnp.zeros((), BF16))
        right = jnp.where(above, state[step, 2], jnp.zeros((), BF16))
        return jnp.concatenate([left, state[step, 1], right], axis=1)

    state[1, 1] = updated(state[0, 1], slope)
    state_copies = send_state(1)

    to(gram_plane.at[0], gram_plane.at[other], gram_send.at[0], gram_recv.at[2], z, other).wait_recv()
    for slot in range(2):
        to(gram_edge, got_gram.at[slot], gram_send.at[0], gram_recv.at[slot], z, other).wait_recv()
    ga, gb = gram_plane[0].astype(F32), gram_plane[1].astype(F32)
    gc = jnp.where(below, got_gram[0].astype(F32), 0.0)
    gd = jnp.where(above, got_gram[1].astype(F32), 0.0)
    mixing[0:128, 0:128] = gc[0:128].astype(BF16)
    mixing[0:128, 128:256] = jnp.zeros((128, 128), BF16)
    mixing[128:256, 0:128] = (gc[128:256] + ga[256:384, 0:128]).astype(BF16)
    mixing[128:256, 128:256] = ga[256:384, 128:256].astype(BF16)
    mixing[256:384, 0:128] = (gc[256:384] + ga[0:128, 0:128] + gb[0:128, 0:128]).astype(BF16)
    mixing[256:384, 128:256] = (ga[0:128, 128:256] + gb[0:128, 128:256]).astype(BF16)
    mixing[384:512, 0:128] = (ga[128:256, 0:128] + gb[128:256, 0:128]).astype(BF16)
    mixing[384:512, 128:256] = (ga[128:256, 128:256] + gb[128:256, 128:256] + gd[256:384]).astype(BF16)
    mixing[512:640, 0:128] = gb[256:384, 0:128].astype(BF16)
    mixing[512:640, 128:256] = (gb[256:384, 128:256] + gd[0:128]).astype(BF16)
    mixing[640:768, 0:128] = jnp.zeros((128, 128), BF16)
    mixing[640:768, 128:256] = gd[128:256].astype(BF16)

    def mixed(step):
        return jnp.dot(full_state(step), mixing[...], preferred_element_type=F32)

    base = slope + mixed(0)
    for step in range(1, ITERS):
        for side, slot in ((0, 0), (1, 2)):
            to(state.at[step, 1], state.at[step, slot], state_send.at[step, side], state_recv.at[step, side], z, other).wait_recv()
        value = updated(state[step, 1], base - mixed(step))
        if step < ITERS - 1:
            state[step + 1, 1] = value
            state_copies += send_state(step + 1)
        else:
            final[...] = value
            final_edge[0] = value[:, :128]
            final_edge[1] = value[:, 128:]

    def band_copy(dy, dx, dl):
        slot = (dy * 4 + dx) * 2 + dl
        return pltpu.make_async_remote_copy(
            final, band_ref.at[core, l, quad], band_send.at[slot], band_recv.at[slot],
            device_id=device(z, (l + dl) % 2, turned(quad, dy, dx), core), device_id_type=MESH)

    def edge_copy(dy, dx, side):
        slot = dy * 4 + dx
        return pltpu.make_async_remote_copy(
            final_edge.at[1 - side], edge_ref.at[core, l, quad], edge_send.at[side, slot], edge_recv.at[l, slot],
            device_id=device(up if side == 0 else down, side, turned(quad, dy, dx), core), device_id_type=MESH)

    steps = [(dy, dx, dl) for dl in range(2) for dy, dx in offsets if (dy, dx, dl) != (0, 0, 0)]
    band_copies = [band_copy(*step) for step in steps]
    edge_copies = [edge_copy(dy, dx, side) for dy, dx in offsets for side in range(2)]
    own_band = pltpu.make_async_copy(final, band_ref.at[core, l, quad], own_sem.at[2])
    own_band.start()
    for copy in edge_copies + band_copies:
        copy.start()

    sibling = (z * 2 + l, quad * 2 + 1 - core)

    def pass_on(k, ref):
        return pltpu.make_async_remote_copy(
            ref.at[core], ref.at[core], pass_send.at[k], pass_recv.at[k], device_id=sibling, device_id_type=MESH)

    for copy in edge_copies:
        copy.wait_send()
    for slot in range(8):
        for side in range(2):
            pltpu.make_async_remote_copy(
                final_edge.at[0], edge_ref.at[core, side, slot], edge_send.at[0, 0], edge_recv.at[side, slot],
                device_id=me, device_id_type=MESH).wait_recv()
    pass_edge = pass_on(0, edge_ref)
    pass_edge.start()
    own_band.wait()
    for copy in band_copies:
        copy.wait()
    pass_band = pass_on(1, band_ref)
    pass_band.start()

    for k, ref in ((0, edge_ref), (1, band_ref)):
        pltpu.make_async_remote_copy(
            ref.at[1 - core], ref.at[1 - core], pass_send.at[k], pass_recv.at[k],
            device_id=me, device_id_type=MESH).wait_recv()
    pass_edge.wait_send()
    pass_band.wait_send()
    own_movie.wait()
    for copy in movie_copies:
        copy.wait()
    for copy in trace_copies + part_copies + gram_copies + state_copies:
        copy.wait_send()


def product_kernel(planes, movie_ref, band_ref, edge_ref, traces_ref, products_ref, gram_ref):
    z, l, quad, core = position()
    outside = jnp.logical_or(jnp.logical_and(l == 0, z == 0), jnp.logical_and(l == 1, z == planes - 1))
    frames = movie_ref.shape[0] * movie_ref.shape[1] * movie_ref.shape[2] * movie_ref.shape[3]
    movie = movie_ref[...].reshape(frames, movie_ref.shape[4])
    plane = band_ref[...].reshape(frames, 256)
    edge = jnp.where(outside, jnp.zeros((), BF16), edge_ref[...].reshape(frames, 128))
    whole = jnp.concatenate([plane, edge], axis=1)
    plane_at = pl.multiple_of((1 - l) * 128, 128)
    edge_at = pl.multiple_of(l * 256, 128)

    def over_frames(left):
        return lax.dot_general(left, whole, (((0,), (0,)), ((), ())), preferred_element_type=F32)

    products = over_frames(movie)
    products_ref[:, pl.ds(plane_at, 256)] = products[:, :256]
    products_ref[:, pl.ds(edge_at, 128)] = products[:, 256:]
    gram = over_frames(whole)
    gram_ref[pl.ds(plane_at, 256), pl.ds(plane_at, 256)] = gram[:256, :256]
    gram_ref[pl.ds(plane_at, 256), pl.ds(edge_at, 128)] = gram[:256, 256:]
    gram_ref[pl.ds(edge_at, 128), pl.ds(plane_at, 256)] = gram[256:, :256]
    gram_ref[pl.ds(edge_at, 128), pl.ds(edge_at, 128)] = gram[256:, 256:]
    for half in range(2):
        traces_ref[half * 64:half * 64 + 64, :] = band_ref[core, half, quad, :, pl.ds(pl.multiple_of(l * 128, 128), 128)]


def body(planes, frames_data, footprints, traces, counts):
    rows, voxels = frames_data.shape
    share = voxels // 16
    half = rows // 2
    hbm = pl.BlockSpec(memory_space=pl.ANY)
    dma = pltpu.SemaphoreType.DMA
    chunks = voxels // CHUNK
    movie, band, edge = pl.pallas_call(
        functools.partial(exchange_kernel, planes),
        name="exchange",
        out_shape=[
            jax.ShapeDtypeStruct((2, 2, 8, half, share), BF16),
            jax.ShapeDtypeStruct((2, 2, 8, half, 256), BF16),
            jax.ShapeDtypeStruct((2, 2, 8, half, 128), BF16),
        ],
        in_specs=[pl.BlockSpec(memory_space=pltpu.SMEM), hbm, hbm, hbm],
        out_specs=[hbm, hbm, hbm],
        scratch_shapes=[
            pltpu.VMEM((voxels, 384), BF16), pltpu.VMEM((2, half, voxels), BF16), pltpu.VMEM((6, rows, 128), BF16),
            pltpu.VMEM((384, 384), F32), pltpu.VMEM((rows + 16, 384), F32),
            pltpu.VMEM((2, half + 8, 256), F32), pltpu.VMEM((2, half + 8, 128), F32),
            pltpu.VMEM((half + 8, 256), F32), pltpu.VMEM((2, half + 8, 128), F32),
            pltpu.VMEM((2, 384, 256), BF16), pltpu.VMEM((384, 128), BF16), pltpu.VMEM((2, 384, 128), BF16),
            pltpu.VMEM((768, 256), BF16),
            pltpu.VMEM((ITERS, 3, half, 256), BF16), pltpu.VMEM((half, 256), BF16), pltpu.VMEM((2, half, 128), BF16),
            dma((chunks, 3)), dma((16,)), dma((16,)), dma((5,)), dma((6,)), dma((3,)), dma((3,)),
            dma((3,)), dma((3,)), dma((ITERS, 2)), dma((ITERS, 2)), dma((16,)), dma((16,)),
            dma((2, 8)), dma((2, 8)), dma((2,)), dma((2,)), dma((3,)),
        ],
        compiler_params=pltpu.CompilerParams(collective_id=0, has_side_effects=True, vmem_limit_bytes=32 << 20),
    )(counts, frames_data.reshape(2, half, voxels), footprints, traces)
    vmem = pl.BlockSpec(memory_space=pltpu.VMEM)
    return pl.pallas_call(
        functools.partial(product_kernel, planes),
        name="products",
        out_shape=[
            jax.ShapeDtypeStruct((rows, 128), BF16),
            jax.ShapeDtypeStruct((share, 384), F32),
            jax.ShapeDtypeStruct((384, 384), F32),
        ],
        in_specs=[vmem, vmem, vmem],
        out_specs=[vmem, vmem, vmem],
        compiler_params=pltpu.CompilerParams(vmem_limit_bytes=32 << 20),
    )(movie, band, edge)


def solution(mesh):
    return jax.shard_map(
        functools.partial(body, mesh.shape["vox"] // 2),
        mesh=mesh,
        in_specs=(P("tm", "vox"), P("vox", None), P("tm", "vox"), P()),
        out_specs=(P("tm", "vox"), P(("vox", "tm"), None), P("vox", None)),
        check_vma=False,
    )
```

time: 338 us -> 68.3 us (0.20)
  waiting for transfers between devices: 230 us -> 0 us
  Pallas kernels: 0 us -> 62.9 us
  starting transfers between devices: 59.4 us -> 0 us
  matrix products: 18 us -> 0 us
  between operations: 14.4 us -> 0.65 us
  local copies, waits for them, and re-layouts: 10.3 us -> 4.52 us
  other arithmetic: 4.59 us -> 0 us
    psum x1 -> x0, waiting for transfers between devices: 207 us -> none  [body(): total, gram = lax.psum((full, gram_part), 'tm')]
    pallas_call x0 -> x2, Pallas kernels: none -> 62.9 us  [the longest x1 60.5 us: body(): pl.pallas_call(functools.partial(exchange_kernel, planes), name='exchange...]
    ppermute x20 -> x0, starting transfers between devices: 59.4 us -> none  [the longest x10 46.5 us: padded_2(): before = lax.ppermute(last, axis, up)]
    ppermute x20 -> x0, waiting for transfers between devices: 22.7 us -> none  [the longest x10 18.3 us: padded_2(): after = lax.ppermute(first, axis, down)]
    dot_general x7 -> x0, matrix products: 18 us -> none  [the longest x4 11.2 us: body(): jnp.dot(resid, blocks, preferred_element_type=jnp.float32)]
    unnamed x6 -> x8, local copies, waits for them, and re-layouts: 9.18 us -> 4.52 us
    reduce_sum x2 -> x0, other arithmetic: 3.91 us -> none  [the longest x1 3.07 us: body(): support = jnp.sum(blocks.astype(jnp.float32), axis=1).astype(jnp.bfloat16)]
  transfers between devices with their start and end apart: 21 -> 0, of which waited for: 10 -> 0; matrix products, arithmetic and copies ran while one was open for 4% -> 0% of each run, Pallas kernels for 0% -> 0%
where the time goes in v1:
time: 68.3 us; the launch traced here: 68 us
  Pallas kernels  62.9 us (92%)
  local copies, waits for them, and re-layouts  4.52 us (7%)
    pallas_call x1, Pallas kernels, body(): pl.pallas_call(functools.partial(exchange_kernel, planes), name='exchange...  60.5 us
    unnamed x8, local copies, waits for them, and re-layouts  4.52 us
    pallas_call x1, Pallas kernels, body(): pl.pallas_call(functools.partial(product_kernel, planes), name='products'...  2.38 us

profile of v1, /device:TPU:1, one launch (start us, length us, event | category | flops | bytes accessed | tf_op | source)
XLA Modules:
  0.0 68.0 jit_solution(14341945064555523205)
XLA Ops:
  0.6 0.0 copy-start
  0.6 1.9 %copy-done = bf16[4096,384]{1,0:T(8,128)(2,1)S(1)} copy-done((bf16[4096,384]{1,0:T(8,128)(2,1)S(1)}, bf16[4096,384]{1,0:T(8,128)(2,1)}, u32[]{:S(2)}) %copy-start) | copy-done | bytes 3145752
  2.5 0.0 copy-start.1
  2.5 1.2 %copy-done.1 = bf16[128,4096]{1,0:T(8,128)(2,1)S(1)} copy-done((bf16[128,4096]{1,0:T(8,128)(2,1)S(1)}, bf16[128,4096]{1,0:T(8,128)(2,1)}, u32[]{:S(2)}) %copy-start.1) | copy-done | bytes 1048600
  3.7 0.0 copy-start.2
  3.7 0.8 %copy-done.2 = bf16[128,128]{1,0:T(8,128)(2,1)S(1)} copy-done((bf16[128,128]{1,0:T(8,128)(2,1)S(1)}, bf16[128,128]{1,0:T(8,128)(2,1)}, u32[]{:S(2)}) %copy-start.2) | copy-done | bytes 32792
  4.5 0.0 copy-start.3
  4.5 0.7 copy-done.3
  5.2 60.5 %exchange.1 = (bf16[2,2,8,64,256]{4,3,2,1,0:T(8,128)(2,1)S(1)}, bf16[2,2,8,64,256]{4,3,2,1,0:T(8,128)(2,1)S(1)}, bf16[2,2,8,64,128]{4,3,2,1,0:T(8,128)(2,1)S(1)}) custom-call(s32[32]{0:T(128)S(1)} %copy-done.3, bf16[2,64,4096]{2,1,0:T(8,128)(2,1)S(1)} %bitcast.1, bf16[4096,384]{1,0:T(8,128)(2,1)S(1)} %copy-done, bf16[128,128]{1,0:T(8,128)(2,1)S(1)} %copy-done.2), custom_call_target="tpu_custom_call" | custom-call | tf_op jit(solution)/shard_map/exchange/pallas_call | solution.py:356
  65.6 2.4 %products.1 = (bf16[128,128]{1,0:T(8,128)(2,1)}, f32[256,384]{1,0:T(8,128)}, f32[384,384]{1,0:T(8,128)}) custom-call(bf16[2,2,8,64,256]{4,3,2,1,0:T(8,128)(2,1)S(1)} %get-tuple-element.6.movie_ref, bf16[2,2,8,64,256]{4,3,2,1,0:T(8,128)(2,1)S(1)} %get-tuple-element.7.band_ref, bf16[2,2,8,64,128]{4,3,2,1,0:T(8,128)(2,1)S(1)} %get-tuple-element.8.edge_ref), custom_call_target="tpu_custom_call" | custom-call | tf_op jit(solution)/shard_map/products/pallas_call | solution.py:381
Async XLA Ops:
  0.6 1.9 %copy-start = (bf16[4096,384]{1,0:T(8,128)(2,1)S(1)}, bf16[4096,384]{1,0:T(8,128)(2,1)}, u32[]{:S(2)}) copy-start(bf16[4096,384]{1,0:T(8,128)(2,1)} %prints_ref.1) | copy-start | bytes 9437188
  2.5 1.2 %copy-start.1 = (bf16[128,4096]{1,0:T(8,128)(2,1)S(1)}, bf16[128,4096]{1,0:T(8,128)(2,1)}, u32[]{:S(2)}) copy-start(bf16[128,4096]{1,0:T(8,128)(2,1)} %param.4) | copy-start | bytes 3145732
  3.7 0.8 %copy-start.2 = (bf16[128,128]{1,0:T(8,128)(2,1)S(1)}, bf16[128,128]{1,0:T(8,128)(2,1)}, u32[]{:S(2)}) copy-start(bf16[128,128]{1,0:T(8,128)(2,1)} %traces_ref.1) | copy-start | bytes 98308
  4.5 0.7 copy-start.3

commit v2 on v1

--- a/solution.py
+++ b/solution.py
@@ -8,7 +8,7 @@
 from jax.sharding import PartitionSpec as P
 
 ITERS = 4
-CHUNK = 512
+CHUNK = 1024
 MESH = pl.DeviceIdType.MESH
 F32 = jnp.float32
 BF16 = jnp.bfloat16
@@ -25,15 +25,15 @@
 
 def exchange_kernel(
     planes,
-    counts_ref, frames_ref, prints_ref, traces_ref,
+    counts_hbm, frames_ref, prints_ref, traces_ref,
     movie_ref, band_ref, edge_ref,
-    prints, frames, tracebuf, gacc, facc,
+    counts_ref, prints, frames, tracebuf, gacc, facc,
     part_plane, part_edge, got_plane, got_edge,
     gram_plane, gram_edge, got_gram, mixing,
     state, final, final_edge,
     load_sem, movie_send, movie_recv, trace_send, trace_recv, part_send, part_recv,
     gram_send, gram_recv, state_send, state_recv, band_send, band_recv,
-    edge_send, edge_recv, pass_send, pass_recv, own_sem,
+    edge_send, edge_recv, pass_send, pass_recv, own_sem, met,
 ):
     z, l, quad, core = position()
     other = 1 - l
@@ -44,25 +44,15 @@
         return (plane * 2 + side, q * 2 + c)
 
     me = device(z, l, quad, core)
+    across = turned(quad, 1, 0)
     offsets = [(dy, dx) for dy in range(2) for dx in range(4)]
+    ring = [(dx, dc) for dx in (1, 3, 2, 0) for dc in range(2) if (dx, dc) != (0, 0)]
     barrier = pltpu.get_barrier_semaphore()
-    greeted = 0
-    for dy, dx in offsets:
-        back = turned(quad, -dy + 2, -dx + 4)
-        for dc in range(2):
-            if (dy, dx, dc) != (0, 0, 0):
-                pl.semaphore_signal(barrier, inc=1, device_id=device(z, l, back, (core + dc) % 2), device_id_type=MESH)
-                greeted += 1
-        pl.semaphore_signal(barrier, inc=1, device_id=device(z, other, back, core), device_id_type=MESH)
-        greeted += 1
-        inward = (z + planes + 2 * l - 1) % planes
-        for side in range(2):
-            pl.semaphore_signal(barrier, inc=1, device_id=device(inward, side, back, core), device_id_type=MESH)
-            greeted += 1
-    far = (z + planes + 1 - 2 * l) % planes
-    for side in range(2):
-        pl.semaphore_signal(barrier, inc=1, device_id=device(far, side, quad, core), device_id_type=MESH)
-        greeted += 1
+    near = [device(z, l, turned(quad, 0, dx), (core + dc) % 2) for dx, dc in ring]
+    near += [device(z, other, quad, core), device(z, l, across, core)]
+    near += [device(plane, side, quad, core) for plane in (up, down) for side in range(2)]
+    for target in near:
+        pl.semaphore_signal(barrier, inc=1, device_id=target, device_id_type=MESH)
 
     rows = prints_ref.shape[0]
     chunks = rows // CHUNK
@@ -77,44 +67,21 @@
             pltpu.make_async_copy(frames_ref.at[:, :, pl.ds(at, CHUNK)], frames.at[:, :, pl.ds(at, CHUNK)], load_sem.at[k, 2]),
         )
 
-    own_trace = pltpu.make_async_copy(traces_ref, tracebuf.at[2 + l], own_sem.at[0])
-    own_trace.start()
+    own_counts = pltpu.make_async_copy(counts_hbm, counts_ref, own_sem.at[3])
+    own_counts.start()
     for k in range(chunks):
         for copy in loads(k):
             copy.start()
+    own_trace = pltpu.make_async_copy(traces_ref, tracebuf.at[2 + l], own_sem.at[0])
+    own_trace.start()
     share = movie_ref.shape[4]
     own_movie = pltpu.make_async_copy(
         frames_ref.at[:, :, pl.ds(pl.multiple_of((quad * 2 + core) * share, share), share)],
         movie_ref.at[core, :, quad], own_sem.at[1])
     own_movie.start()
-
-    pl.semaphore_wait(barrier, greeted)
-
-    def trace_copy(k, plane, side, slot):
-        return pltpu.make_async_remote_copy(
-            traces_ref, tracebuf.at[slot], trace_send.at[k], trace_recv.at[slot],
-            device_id=device(plane, side, quad, core), device_id_type=MESH)
-
-    trace_copies = [
-        trace_copy(0, z, other, 2 + l),
-        trace_copy(1, up, 0, l), trace_copy(2, up, 1, l),
-        trace_copy(3, down, 0, 4 + l), trace_copy(4, down, 1, 4 + l),
-    ]
-    for copy in trace_copies:
-        copy.start()
-
-    movie_copies = []
-    for dc in range(2):
-        for dy, dx in offsets:
-            if (dy, dx, dc) != (0, 0, 0):
-                q, c = turned(quad, dy, dx), (core + dc) % 2
-                slot = (dy * 4 + dx) * 2 + dc
-                movie_copies.append(pltpu.make_async_remote_copy(
-                    frames_ref.at[:, :, pl.ds(pl.multiple_of((q * 2 + c) * share, share), share)],
-                    movie_ref.at[core, :, quad], movie_send.at[slot], movie_recv.at[slot],
-                    device_id=device(z, l, q, c), device_id_type=MESH))
-    for copy in movie_copies:
-        copy.start()
+    gacc[...] = jnp.zeros_like(gacc)
+    facc[...] = jnp.zeros_like(facc)
+    own_counts.wait()
 
     def number(tile):
         inside = jnp.logical_and(tile >= 0, tile < 2 * planes)
@@ -122,7 +89,6 @@
 
     numbers = [number(2 * z - 2 + s) for s in range(6)]
     edge_number = jnp.where(l == 0, numbers[1], numbers[4])
-
     lane = lax.broadcasted_iota(jnp.int32, (1, 128), 1)
     row = lax.broadcasted_iota(jnp.int32, (128, 1), 0)
     live_rows = jnp.concatenate(
@@ -130,25 +96,57 @@
     live_lanes = [(lane < n).astype(F32) for n in numbers]
     own_live = jnp.concatenate([live_lanes[2], live_lanes[3]], axis=1)
 
-    gacc[...] = jnp.zeros_like(gacc)
-    facc[...] = jnp.zeros_like(facc)
-
     def chunk_step(k, carry):
         for copy in loads(k):
             copy.wait()
         at = pl.multiple_of(k * CHUNK, CHUNK)
         block = prints[pl.ds(at, CHUNK), :]
-        turned_block = block.T
-        support = jnp.sum(turned_block.astype(F32) * live_rows, axis=0, keepdims=True).astype(BF16)
+        flipped = block.T
+        support = jnp.sum(flipped.astype(F32) * live_rows, axis=0, keepdims=True).astype(BF16)
         left = jnp.concatenate(
-            [frames[0, :, pl.ds(at, CHUNK)], frames[1, :, pl.ds(at, CHUNK)],
+            [flipped[256:384], frames[0, :, pl.ds(at, CHUNK)], frames[1, :, pl.ds(at, CHUNK)],
              jnp.broadcast_to(support, (16, CHUNK))], axis=0)
-        facc[...] += jnp.dot(left, block, preferred_element_type=F32)
-        gacc[...] += jnp.dot(turned_block, block, preferred_element_type=F32)
+        edge = jnp.dot(left, block[:, 256:384], preferred_element_type=F32)
+        gacc[256:384, 256:384] += edge[0:128]
+        facc[:, 256:384] += edge[128:272]
+        left = jnp.concatenate([left, flipped[0:256]], axis=0)
+        plane = jnp.dot(left, block[:, 0:256], preferred_element_type=F32)
+        gacc[256:384, 0:256] += plane[0:128]
+        facc[:, 0:256] += plane[128:272]
+        gacc[0:256, 0:256] += plane[272:528]
         return carry
 
-    lax.fori_loop(0, chunks, chunk_step, 0)
-
+    chunk_step(0, 0)
+    pl.semaphore_wait(barrier, len(near))
+    pl.semaphore_signal(met, inc=1, device_id=device(z, l, across, core), device_id_type=MESH)
+
+    def to(src, dst, send, recv, plane, side, q=None):
+        return pltpu.make_async_remote_copy(
+            src, dst, send, recv, device_id=device(plane, side, quad if q is None else q, core), device_id_type=MESH)
+
+    trace_copies = [
+        to(traces_ref, tracebuf.at[slot], trace_send.at[k], trace_recv.at[slot], plane, side)
+        for k, (plane, side, slot) in enumerate(
+            [(z, other, 2 + l), (up, 0, l), (up, 1, l), (down, 0, 4 + l), (down, 1, 4 + l)])
+    ]
+    for copy in trace_copies:
+        copy.start()
+
+    def movie_copy(dy, dx, dc):
+        q, c = turned(quad, dy, dx), (core + dc) % 2
+        slot = (dy * 4 + dx) * 2 + dc
+        return pltpu.make_async_remote_copy(
+            frames_ref.at[:, :, pl.ds(pl.multiple_of((q * 2 + c) * share, share), share)],
+            movie_ref.at[core, :, quad], movie_send.at[slot], movie_recv.at[slot],
+            device_id=device(z, l, q, c), device_id_type=MESH)
+
+    movie_copies = [movie_copy(0, dx, dc) for dx, dc in ring]
+    for copy in movie_copies:
+        copy.start()
+
+    lax.fori_loop(1, chunks, chunk_step, 0)
+
+    gacc[0:256, 256:384] = gacc[256:384, 0:256].T
     gram = gacc[...]
     high = gram.astype(BF16)
     low = (gram - high.astype(F32)).astype(BF16)
@@ -156,15 +154,8 @@
     gram_edge[...] = high[:, 256:]
 
     own_trace.wait()
-
-    def trace_arrival(slot):
-        pltpu.make_async_remote_copy(
-            traces_ref, tracebuf.at[slot], trace_send.at[0], trace_recv.at[slot],
-            device_id=me, device_id_type=MESH).wait_recv()
-
-    for slot in (0, 1, 4, 5):
-        trace_arrival(slot)
-    trace_arrival(2 + other)
+    for slot in (0, 1, 4, 5, 2 + other):
+        to(traces_ref, tracebuf.at[slot], trace_send.at[0], trace_recv.at[slot], z, other).wait_recv()
 
     def trace(slot, live):
         return (tracebuf[slot].astype(F32) * live).astype(BF16)
@@ -178,20 +169,18 @@
         piece = jnp.concatenate([parts[half * 64:half * 64 + 64], reach], axis=0)
         part_plane[half] = piece[:, :256]
         part_edge[half] = piece[:, 256:]
-
-    def to(src, dst, send, recv, plane, side):
-        return pltpu.make_async_remote_copy(
-            src, dst, send, recv, device_id=device(plane, side, quad, core), device_id_type=MESH)
+    pl.semaphore_wait(met, 1)
 
     part_copies = [
         to(part_plane.at[other], got_plane, part_send.at[0], part_recv.at[2], z, other),
+        to(part_edge.at[other], got_edge.at[other], part_send.at[2], part_recv.at[other], outward, other),
         to(part_edge.at[l], got_edge.at[other], part_send.at[1], part_recv.at[other], outward, l),
-        to(part_edge.at[other], got_edge.at[other], part_send.at[2], part_recv.at[other], outward, other),
     ]
+    own_rows = pl.ds(pl.multiple_of(core * 192, 64), 192)
     gram_copies = [
-        to(gram_plane.at[l], gram_plane.at[l], gram_send.at[0], gram_recv.at[2], z, other),
-        to(gram_edge, got_gram.at[other], gram_send.at[1], gram_recv.at[other], outward, l),
-        to(gram_edge, got_gram.at[other], gram_send.at[2], gram_recv.at[other], outward, other),
+        to(gram_plane.at[l, own_rows], gram_plane.at[l, own_rows], gram_send.at[0], gram_recv.at[2], z, other, across),
+        to(gram_edge.at[own_rows], got_gram.at[other, own_rows], gram_send.at[2], gram_recv.at[other], outward, other, across),
+        to(gram_edge.at[own_rows], got_gram.at[other, own_rows], gram_send.at[1], gram_recv.at[other], outward, l),
     ]
     for copy in part_copies + gram_copies:
         copy.start()
@@ -231,9 +220,32 @@
     state[1, 1] = updated(state[0, 1], slope)
     state_copies = send_state(1)
 
-    to(gram_plane.at[0], gram_plane.at[other], gram_send.at[0], gram_recv.at[2], z, other).wait_recv()
-    for slot in range(2):
-        to(gram_edge, got_gram.at[slot], gram_send.at[0], gram_recv.at[slot], z, other).wait_recv()
+    late_movie = [movie_copy(1, dx, dc) for dx in (0, 2, 1, 3) for dc in range(2)]
+    for copy in late_movie:
+        copy.start()
+    movie_copies += late_movie
+
+    sibling = (z * 2 + l, quad * 2 + 1 - core)
+
+    def gram_pass(k, refs):
+        ref = refs(own_rows)
+        return pltpu.make_async_remote_copy(
+            ref, ref, pass_send.at[k], pass_recv.at[k], device_id=sibling, device_id_type=MESH)
+
+    gram_parts = [
+        (2, lambda part: gram_plane.at[other, part]),
+        (0, lambda part: got_gram.at[0, part]),
+        (1, lambda part: got_gram.at[1, part]),
+    ]
+    passes = []
+    for k, refs in gram_parts:
+        to(refs(own_rows), refs(own_rows), gram_send.at[0], gram_recv.at[k], z, other).wait_recv()
+        passes.append(gram_pass(k, refs))
+        passes[-1].start()
+    its_rows = pl.ds(pl.multiple_of((1 - core) * 192, 64), 192)
+    for k, refs in gram_parts:
+        pltpu.make_async_remote_copy(
+            refs(its_rows), refs(its_rows), pass_send.at[k], pass_recv.at[k], device_id=sibling, device_id_type=MESH).wait_recv()
     ga, gb = gram_plane[0].astype(F32), gram_plane[1].astype(F32)
     gc = jnp.where(below, got_gram[0].astype(F32), 0.0)
     gd = jnp.where(above, got_gram[1].astype(F32), 0.0)
@@ -278,45 +290,50 @@
             final_edge.at[1 - side], edge_ref.at[core, l, quad], edge_send.at[side, slot], edge_recv.at[l, slot],
             device_id=device(up if side == 0 else down, side, turned(quad, dy, dx), core), device_id_type=MESH)
 
-    steps = [(dy, dx, dl) for dl in range(2) for dy, dx in offsets if (dy, dx, dl) != (0, 0, 0)]
-    band_copies = [band_copy(*step) for step in steps]
-    edge_copies = [edge_copy(dy, dx, side) for dy, dx in offsets for side in range(2)]
     own_band = pltpu.make_async_copy(final, band_ref.at[core, l, quad], own_sem.at[2])
     own_band.start()
-    for copy in edge_copies + band_copies:
-        copy.start()
-
-    sibling = (z * 2 + l, quad * 2 + 1 - core)
-
-    def pass_on(k, ref):
-        return pltpu.make_async_remote_copy(
-            ref.at[core], ref.at[core], pass_send.at[k], pass_recv.at[k], device_id=sibling, device_id_type=MESH)
-
-    for copy in edge_copies:
+    batches = [("edge", 1, 0), ("band", 1, 0), ("edge", 1, 1), ("band", 0, 1), ("edge", 0, 0), ("band", 1, 1), ("edge", 0, 1), ("band", 0, 0)]
+    band_copies, edge_copies = [], []
+    for kind, dy, side in batches:
+        for dx in (2, 1, 3, 0):
+            if kind == "edge":
+                edge_copies.append(edge_copy(dy, dx, side))
+                edge_copies[-1].start()
+            elif (dy, dx, side) != (0, 0, 0):
+                band_copies.append(band_copy(dy, dx, side))
+                band_copies[-1].start()
+
+    def row_of(kind, dy, side, c):
+        yh = (quad // 4 + dy) % 2
+        if kind == "edge":
+            return edge_ref.at[c, side, pl.ds(yh * 4, 4)]
+        return band_ref.at[c, (l + side) % 2, pl.ds(yh * 4, 4)]
+
+    for k, (kind, dy, side) in enumerate(batches):
+        for dx in range(4):
+            slot = dy * 4 + dx
+            if kind == "edge":
+                pltpu.make_async_remote_copy(
+                    final_edge.at[0], edge_ref.at[core, side, slot], edge_send.at[0, 0], edge_recv.at[side, slot],
+                    device_id=sibling, device_id_type=MESH).wait_recv()
+            elif (dy, dx, side) != (0, 0, 0):
+                band_copy(dy, dx, side).wait_recv()
+            else:
+                own_band.wait()
+        ref = row_of(kind, dy, side, core)
+        passes.append(pltpu.make_async_remote_copy(
+            ref, ref, pass_send.at[3 + k], pass_recv.at[3 + k], device_id=sibling, device_id_type=MESH))
+        passes[-1].start()
+    for copy in trace_copies + part_copies + gram_copies + state_copies + edge_copies + band_copies:
         copy.wait_send()
-    for slot in range(8):
-        for side in range(2):
-            pltpu.make_async_remote_copy(
-                final_edge.at[0], edge_ref.at[core, side, slot], edge_send.at[0, 0], edge_recv.at[side, slot],
-                device_id=me, device_id_type=MESH).wait_recv()
-    pass_edge = pass_on(0, edge_ref)
-    pass_edge.start()
-    own_band.wait()
-    for copy in band_copies:
-        copy.wait()
-    pass_band = pass_on(1, band_ref)
-    pass_band.start()
-
-    for k, ref in ((0, edge_ref), (1, band_ref)):
-        pltpu.make_async_remote_copy(
-            ref.at[1 - core], ref.at[1 - core], pass_send.at[k], pass_recv.at[k],
-            device_id=me, device_id_type=MESH).wait_recv()
-    pass_edge.wait_send()
-    pass_band.wait_send()
     own_movie.wait()
     for copy in movie_copies:
         copy.wait()
-    for copy in trace_copies + part_copies + gram_copies + state_copies:
+    for k, (kind, dy, side) in enumerate(batches):
+        ref = row_of(kind, dy, side, 1 - core)
+        pltpu.make_async_remote_copy(
+            ref, ref, pass_send.at[3 + k], pass_recv.at[3 + k], device_id=sibling, device_id_type=MESH).wait_recv()
+    for copy in passes:
         copy.wait_send()
 
 
@@ -361,9 +378,10 @@
             jax.ShapeDtypeStruct((2, 2, 8, half, 256), BF16),
             jax.ShapeDtypeStruct((2, 2, 8, half, 128), BF16),
         ],
-        in_specs=[pl.BlockSpec(memory_space=pltpu.SMEM), hbm, hbm, hbm],
+        in_specs=[hbm, hbm, hbm, hbm],
         out_specs=[hbm, hbm, hbm],
         scratch_shapes=[
+            pltpu.SMEM((counts.shape[0],), jnp.int32),
             pltpu.VMEM((voxels, 384), BF16), pltpu.VMEM((2, half, voxels), BF16), pltpu.VMEM((6, rows, 128), BF16),
             pltpu.VMEM((384, 384), F32), pltpu.VMEM((rows + 16, 384), F32),
             pltpu.VMEM((2, half + 8, 256), F32), pltpu.VMEM((2, half + 8, 128), F32),
@@ -373,10 +391,10 @@
             pltpu.VMEM((ITERS, 3, half, 256), BF16), pltpu.VMEM((half, 256), BF16), pltpu.VMEM((2, half, 128), BF16),
             dma((chunks, 3)), dma((16,)), dma((16,)), dma((5,)), dma((6,)), dma((3,)), dma((3,)),
             dma((3,)), dma((3,)), dma((ITERS, 2)), dma((ITERS, 2)), dma((16,)), dma((16,)),
-            dma((2, 8)), dma((2, 8)), dma((2,)), dma((2,)), dma((3,)),
+            dma((2, 8)), dma((2, 8)), dma((11,)), dma((11,)), dma((4,)), pltpu.SemaphoreType.REGULAR,
         ],
         compiler_params=pltpu.CompilerParams(collective_id=0, has_side_effects=True, vmem_limit_bytes=32 << 20),
-    )(counts, frames_data.reshape(2, half, voxels), footprints, traces)
+    )(*[pltpu.with_memory_space_constraint(v, pltpu.HBM) for v in (counts, frames_data.reshape(2, half, voxels), footprints, traces)])
     vmem = pl.BlockSpec(memory_space=pltpu.VMEM)
     return pl.pallas_call(
         functools.partial(product_kernel, planes),

time: 68.3 us -> 54.3 us (0.80)
  Pallas kernels: 62.9 us -> 53.6 us
  local copies, waits for them, and re-layouts: 4.52 us -> 0 us
    pallas_call x1, Pallas kernels: 60.5 us -> 51.2 us  [body(): pl.pallas_call(functools.partial(exchange_kernel, planes), name='exchange...]
    unnamed x8 -> x0, local copies, waits for them, and re-layouts: 4.52 us -> none
where the time goes in v2:
time: 54.3 us; the launch traced here: 54.2 us
  Pallas kernels  53.6 us (99%)
  between operations  0.64 us (1%)
    pallas_call x1, Pallas kernels, body(): pl.pallas_call(functools.partial(exchange_kernel, planes), name='exchange...  51.2 us
    pallas_call x1, Pallas kernels, body(): pl.pallas_call(functools.partial(product_kernel, planes), name='products'...  2.37 us

profile of v2, /device:TPU:1, one launch (start us, length us, event | category | flops | bytes accessed | tf_op | source)
XLA Modules:
  0.0 54.2 jit_solution(5954231575563780730)
XLA Ops:
  0.6 51.2 %exchange.1 = (bf16[2,2,8,64,256]{4,3,2,1,0:T(8,128)(2,1)S(1)}, bf16[2,2,8,64,256]{4,3,2,1,0:T(8,128)(2,1)S(1)}, bf16[2,2,8,64,128]{4,3,2,1,0:T(8,128)(2,1)S(1)}) custom-call(s32[32]{0:T(128)} %counts_hbm.1, bf16[2,64,4096]{2,1,0:T(8,128)(2,1)} %bitcast.1, bf16[4096,384]{1,0:T(8,128)(2,1)} %prints_ref.1, bf16[128,128]{1,0:T(8,128)(2,1)} %traces_ref.1), custom_call_target="tpu_custom_call" | custom-call | tf_op jit(solution)/shard_map/exchange/pallas_call | solution.py:373
  51.9 2.4 %products.1 = (bf16[128,128]{1,0:T(8,128)(2,1)}, f32[256,384]{1,0:T(8,128)}, f32[384,384]{1,0:T(8,128)}) custom-call(bf16[2,2,8,64,256]{4,3,2,1,0:T(8,128)(2,1)S(1)} %get-tuple-element.6.movie_ref, bf16[2,2,8,64,256]{4,3,2,1,0:T(8,128)(2,1)S(1)} %get-tuple-element.7.band_ref, bf16[2,2,8,64,128]{4,3,2,1,0:T(8,128)(2,1)S(1)} %get-tuple-element.8.edge_ref), custom_call_target="tpu_custom_call" | custom-call | tf_op jit(solution)/shard_map/products/pallas_call | solution.py:399

commit v3 on v2

--- a/solution.py
+++ b/solution.py
@@ -26,7 +26,7 @@
 def exchange_kernel(
     planes,
     counts_hbm, frames_ref, prints_ref, traces_ref,
-    movie_ref, band_ref, edge_ref,
+    movie_ref, band_ref, edge_ref, products_ref, gram_ref,
     counts_ref, prints, frames, tracebuf, gacc, facc,
     part_plane, part_edge, got_plane, got_edge,
     gram_plane, gram_edge, got_gram, mixing,
@@ -39,6 +39,15 @@
     other = 1 - l
     up, down = (z + 1) % planes, (z + planes - 1) % planes
     outward = (z + planes - 1 + 2 * l) % planes
+    below, above = z > 0, z < planes - 1
+    beside = jnp.where(l == 0, z, planes - 1 - z) > 0
+    always = None
+
+    def given(condition, act):
+        if condition is None:
+            act()
+        else:
+            pl.when(condition)(act)
 
     def device(plane, side, q, c):
         return (plane * 2 + side, q * 2 + c)
@@ -50,9 +59,8 @@
     barrier = pltpu.get_barrier_semaphore()
     near = [device(z, l, turned(quad, 0, dx), (core + dc) % 2) for dx, dc in ring]
     near += [device(z, other, quad, core), device(z, l, across, core)]
-    near += [device(plane, side, quad, core) for plane in (up, down) for side in range(2)]
-    for target in near:
-        pl.semaphore_signal(barrier, inc=1, device_id=target, device_id_type=MESH)
+    near = [(always, target) for target in near]
+    near += [(there, device(plane, side, quad, core)) for there, plane in ((above, up), (below, down)) for side in range(2)]
 
     rows = prints_ref.shape[0]
     chunks = rows // CHUNK
@@ -79,6 +87,17 @@
         frames_ref.at[:, :, pl.ds(pl.multiple_of((quad * 2 + core) * share, share), share)],
         movie_ref.at[core, :, quad], own_sem.at[1])
     own_movie.start()
+    for there, target in near:
+        given(there, functools.partial(pl.semaphore_signal, barrier, inc=1, device_id=target, device_id_type=MESH))
+
+    @pl.when(jnp.logical_not(below))
+    def _():
+        tracebuf[0:2] = jnp.zeros((2,) + tracebuf.shape[1:], BF16)
+
+    @pl.when(jnp.logical_not(above))
+    def _():
+        tracebuf[4:6] = jnp.zeros((2,) + tracebuf.shape[1:], BF16)
+
     gacc[...] = jnp.zeros_like(gacc)
     facc[...] = jnp.zeros_like(facc)
     own_counts.wait()
@@ -117,20 +136,22 @@
         return carry
 
     chunk_step(0, 0)
-    pl.semaphore_wait(barrier, len(near))
+    pl.semaphore_wait(barrier, len(near) - 4 + 2 * below.astype(jnp.int32) + 2 * above.astype(jnp.int32))
     pl.semaphore_signal(met, inc=1, device_id=device(z, l, across, core), device_id_type=MESH)
 
     def to(src, dst, send, recv, plane, side, q=None):
         return pltpu.make_async_remote_copy(
             src, dst, send, recv, device_id=device(plane, side, quad if q is None else q, core), device_id_type=MESH)
 
-    trace_copies = [
-        to(traces_ref, tracebuf.at[slot], trace_send.at[k], trace_recv.at[slot], plane, side)
-        for k, (plane, side, slot) in enumerate(
-            [(z, other, 2 + l), (up, 0, l), (up, 1, l), (down, 0, 4 + l), (down, 1, 4 + l)])
-    ]
-    for copy in trace_copies:
-        copy.start()
+    sent = []
+
+    def send(there, copy):
+        given(there, copy.start)
+        sent.append((there, copy))
+
+    for k, (there, plane, side, slot) in enumerate(
+            [(always, z, other, 2 + l), (above, up, 0, l), (above, up, 1, l), (below, down, 0, 4 + l), (below, down, 1, 4 + l)]):
+        send(there, to(traces_ref, tracebuf.at[slot], trace_send.at[k], trace_recv.at[slot], plane, side))
 
     def movie_copy(dy, dx, dc):
         q, c = turned(quad, dy, dx), (core + dc) % 2
@@ -140,10 +161,6 @@
             movie_ref.at[core, :, quad], movie_send.at[slot], movie_recv.at[slot],
             device_id=device(z, l, q, c), device_id_type=MESH)
 
-    movie_copies = [movie_copy(0, dx, dc) for dx, dc in ring]
-    for copy in movie_copies:
-        copy.start()
-
     lax.fori_loop(1, chunks, chunk_step, 0)
 
     gacc[0:256, 256:384] = gacc[256:384, 0:256].T
@@ -154,8 +171,8 @@
     gram_edge[...] = high[:, 256:]
 
     own_trace.wait()
-    for slot in (0, 1, 4, 5, 2 + other):
-        to(traces_ref, tracebuf.at[slot], trace_send.at[0], trace_recv.at[slot], z, other).wait_recv()
+    for there, slot in ((below, 0), (below, 1), (above, 4), (above, 5), (always, 2 + other)):
+        given(there, to(traces_ref, tracebuf.at[slot], trace_send.at[0], trace_recv.at[slot], z, other).wait_recv)
 
     def trace(slot, live):
         return (tracebuf[slot].astype(F32) * live).astype(BF16)
@@ -171,18 +188,15 @@
         part_edge[half] = piece[:, 256:]
     pl.semaphore_wait(met, 1)
 
-    part_copies = [
-        to(part_plane.at[other], got_plane, part_send.at[0], part_recv.at[2], z, other),
-        to(part_edge.at[other], got_edge.at[other], part_send.at[2], part_recv.at[other], outward, other),
-        to(part_edge.at[l], got_edge.at[other], part_send.at[1], part_recv.at[other], outward, l),
-    ]
+    send(always, to(part_plane.at[other], got_plane, part_send.at[0], part_recv.at[2], z, other))
+    send(beside, to(part_edge.at[other], got_edge.at[other], part_send.at[2], part_recv.at[other], outward, other))
+    send(beside, to(part_edge.at[l], got_edge.at[other], part_send.at[1], part_recv.at[other], outward, l))
     own_rows = pl.ds(pl.multiple_of(core * 192, 64), 192)
-    gram_copies = [
-        to(gram_plane.at[l, own_rows], gram_plane.at[l, own_rows], gram_send.at[0], gram_recv.at[2], z, other, across),
-        to(gram_edge.at[own_rows], got_gram.at[other, own_rows], gram_send.at[2], gram_recv.at[other], outward, other, across),
-        to(gram_edge.at[own_rows], got_gram.at[other, own_rows], gram_send.at[1], gram_recv.at[other], outward, l),
-    ]
-    for copy in part_copies + gram_copies:
+    send(always, to(gram_plane.at[l, own_rows], gram_plane.at[l, own_rows], gram_send.at[0], gram_recv.at[2], z, other, across))
+    send(beside, to(gram_edge.at[own_rows], got_gram.at[other, own_rows], gram_send.at[2], gram_recv.at[other], outward, other, across))
+    send(beside, to(gram_edge.at[own_rows], got_gram.at[other, own_rows], gram_send.at[1], gram_recv.at[other], outward, l))
+    movie_copies = [movie_copy(0, dx, dc) for dx, dc in ring]
+    for copy in movie_copies:
         copy.start()
 
     mine = pl.ds(pl.multiple_of(l * 64, 64), 64)
@@ -191,9 +205,8 @@
         state[0, s // 2, :, (s % 2) * 128:(s % 2) * 128 + 128] = value
 
     to(part_plane.at[0], got_plane, part_send.at[0], part_recv.at[2], z, other).wait_recv()
-    for slot in range(2):
-        to(part_edge.at[0], got_edge.at[slot], part_send.at[0], part_recv.at[slot], z, other).wait_recv()
-    below, above = z > 0, z < planes - 1
+    for there, slot in ((below, 0), (above, 1)):
+        given(there, to(part_edge.at[0], got_edge.at[slot], part_send.at[0], part_recv.at[slot], z, other).wait_recv)
     total = part_plane[l] + got_plane[...] + jnp.concatenate(
         [jnp.where(below, got_edge[0], 0.0), jnp.where(above, got_edge[1], 0.0)], axis=1)
     slope = total[0:64]
@@ -204,21 +217,11 @@
         return (value * own_live).astype(BF16)
 
     def send_state(step):
-        copies = [
-            to(state.at[step, 1], state.at[step, 0], state_send.at[step, 0], state_recv.at[step, 0], up, l),
-            to(state.at[step, 1], state.at[step, 2], state_send.at[step, 1], state_recv.at[step, 1], down, l),
-        ]
-        for copy in copies:
-            copy.start()
-        return copies
-
-    def full_state(step):
-        left = jnp.where(below, state[step, 0], jnp.zeros((), BF16))
-        right = jnp.where(above, state[step, 2], jnp.zeros((), BF16))
-        return jnp.concatenate([left, state[step, 1], right], axis=1)
+        send(above, to(state.at[step, 1], state.at[step, 0], state_send.at[step, 0], state_recv.at[step, 0], up, l))
+        send(below, to(state.at[step, 1], state.at[step, 2], state_send.at[step, 1], state_recv.at[step, 1], down, l))
 
     state[1, 1] = updated(state[0, 1], slope)
-    state_copies = send_state(1)
+    send_state(1)
 
     late_movie = [movie_copy(1, dx, dc) for dx in (0, 2, 1, 3) for dc in range(2)]
     for copy in late_movie:
@@ -233,19 +236,17 @@
             ref, ref, pass_send.at[k], pass_recv.at[k], device_id=sibling, device_id_type=MESH)
 
     gram_parts = [
-        (2, lambda part: gram_plane.at[other, part]),
-        (0, lambda part: got_gram.at[0, part]),
-        (1, lambda part: got_gram.at[1, part]),
+        (always, 2, lambda part: gram_plane.at[other, part]),
+        (below, 0, lambda part: got_gram.at[0, part]),
+        (above, 1, lambda part: got_gram.at[1, part]),
     ]
-    passes = []
-    for k, refs in gram_parts:
-        to(refs(own_rows), refs(own_rows), gram_send.at[0], gram_recv.at[k], z, other).wait_recv()
-        passes.append(gram_pass(k, refs))
-        passes[-1].start()
+    for there, k, refs in gram_parts:
+        given(there, to(refs(own_rows), refs(own_rows), gram_send.at[0], gram_recv.at[k], z, other).wait_recv)
+        send(there, gram_pass(k, refs))
     its_rows = pl.ds(pl.multiple_of((1 - core) * 192, 64), 192)
-    for k, refs in gram_parts:
-        pltpu.make_async_remote_copy(
-            refs(its_rows), refs(its_rows), pass_send.at[k], pass_recv.at[k], device_id=sibling, device_id_type=MESH).wait_recv()
+    for there, k, refs in gram_parts:
+        given(there, pltpu.make_async_remote_copy(
+            refs(its_rows), refs(its_rows), pass_send.at[k], pass_recv.at[k], device_id=sibling, device_id_type=MESH).wait_recv)
     ga, gb = gram_plane[0].astype(F32), gram_plane[1].astype(F32)
     gc = jnp.where(below, got_gram[0].astype(F32), 0.0)
     gd = jnp.where(above, got_gram[1].astype(F32), 0.0)
@@ -262,17 +263,24 @@
     mixing[640:768, 0:128] = jnp.zeros((128, 128), BF16)
     mixing[640:768, 128:256] = gd[128:256].astype(BF16)
 
-    def mixed(step):
-        return jnp.dot(full_state(step), mixing[...], preferred_element_type=F32)
-
-    base = slope + mixed(0)
+    def mixed_own(step):
+        return jnp.dot(state[step, 1], mixing[256:512], preferred_element_type=F32)
+
+    def mixed_next(step):
+        left = jnp.where(below, state[step, 0], jnp.zeros((), BF16))
+        right = jnp.where(above, state[step, 2], jnp.zeros((), BF16))
+        return (jnp.dot(left, mixing[0:256], preferred_element_type=F32)
+                + jnp.dot(right, mixing[512:768], preferred_element_type=F32))
+
+    base = slope + mixed_own(0) + mixed_next(0)
     for step in range(1, ITERS):
-        for side, slot in ((0, 0), (1, 2)):
-            to(state.at[step, 1], state.at[step, slot], state_send.at[step, side], state_recv.at[step, side], z, other).wait_recv()
-        value = updated(state[step, 1], base - mixed(step))
+        partial = base - mixed_own(step)
+        for there, side, slot in ((below, 0, 0), (above, 1, 2)):
+            given(there, to(state.at[step, 1], state.at[step, slot], state_send.at[step, side], state_recv.at[step, side], z, other).wait_recv)
+        value = updated(state[step, 1], partial - mixed_next(step))
         if step < ITERS - 1:
             state[step + 1, 1] = value
-            state_copies += send_state(step + 1)
+            send_state(step + 1)
         else:
             final[...] = value
             final_edge[0] = value[:, :128]
@@ -293,15 +301,12 @@
     own_band = pltpu.make_async_copy(final, band_ref.at[core, l, quad], own_sem.at[2])
     own_band.start()
     batches = [("edge", 1, 0), ("band", 1, 0), ("edge", 1, 1), ("band", 0, 1), ("edge", 0, 0), ("band", 1, 1), ("edge", 0, 1), ("band", 0, 0)]
-    band_copies, edge_copies = [], []
     for kind, dy, side in batches:
         for dx in (2, 1, 3, 0):
             if kind == "edge":
-                edge_copies.append(edge_copy(dy, dx, side))
-                edge_copies[-1].start()
+                send(above if side == 0 else below, edge_copy(dy, dx, side))
             elif (dy, dx, side) != (0, 0, 0):
-                band_copies.append(band_copy(dy, dx, side))
-                band_copies[-1].start()
+                send(always, band_copy(dy, dx, side))
 
     def row_of(kind, dy, side, c):
         yh = (quad // 4 + dy) % 2
@@ -309,56 +314,63 @@
             return edge_ref.at[c, side, pl.ds(yh * 4, 4)]
         return band_ref.at[c, (l + side) % 2, pl.ds(yh * 4, 4)]
 
+    own_movie.wait()
+    for copy in movie_copies:
+        copy.wait_recv()
     for k, (kind, dy, side) in enumerate(batches):
+        there = beside if kind == "edge" else always
         for dx in range(4):
             slot = dy * 4 + dx
             if kind == "edge":
-                pltpu.make_async_remote_copy(
+                given(there, pltpu.make_async_remote_copy(
                     final_edge.at[0], edge_ref.at[core, side, slot], edge_send.at[0, 0], edge_recv.at[side, slot],
-                    device_id=sibling, device_id_type=MESH).wait_recv()
+                    device_id=sibling, device_id_type=MESH).wait_recv)
             elif (dy, dx, side) != (0, 0, 0):
                 band_copy(dy, dx, side).wait_recv()
             else:
                 own_band.wait()
         ref = row_of(kind, dy, side, core)
-        passes.append(pltpu.make_async_remote_copy(
+        send(there, pltpu.make_async_remote_copy(
             ref, ref, pass_send.at[3 + k], pass_recv.at[3 + k], device_id=sibling, device_id_type=MESH))
-        passes[-1].start()
-    for copy in trace_copies + part_copies + gram_copies + state_copies + edge_copies + band_copies:
+
+    partial_products(beside, movie_ref.at[core], band_ref.at[core], edge_ref.at[core], products_ref, gram_ref)
+
+    for there, copy in sent:
+        given(there, copy.wait_send)
+    for copy in movie_copies:
         copy.wait_send()
-    own_movie.wait()
-    for copy in movie_copies:
-        copy.wait()
     for k, (kind, dy, side) in enumerate(batches):
         ref = row_of(kind, dy, side, 1 - core)
-        pltpu.make_async_remote_copy(
-            ref, ref, pass_send.at[3 + k], pass_recv.at[3 + k], device_id=sibling, device_id_type=MESH).wait_recv()
-    for copy in passes:
-        copy.wait_send()
-
-
-def product_kernel(planes, movie_ref, band_ref, edge_ref, traces_ref, products_ref, gram_ref):
+        given(beside if kind == "edge" else always, pltpu.make_async_remote_copy(
+            ref, ref, pass_send.at[3 + k], pass_recv.at[3 + k], device_id=sibling, device_id_type=MESH).wait_recv)
+
+
+def partial_products(beside, movie_ref, band_ref, edge_ref, products_ref, gram_ref):
+    frames = movie_ref.shape[0] * movie_ref.shape[1] * movie_ref.shape[2]
+    movie = movie_ref[...].reshape(frames, movie_ref.shape[3])
+    plane = band_ref[...].reshape(frames, 256)
+    edge = jnp.where(beside, edge_ref[...].reshape(frames, 128), jnp.zeros((), BF16))
+    whole = jnp.concatenate([plane, edge], axis=1)
+
+    def over_frames(left):
+        return lax.dot_general(left, whole, (((0,), (0,)), ((), ())), preferred_element_type=F32)
+
+    products_ref[...] = over_frames(movie)
+    gram_ref[...] = over_frames(whole)
+
+
+def product_kernel(planes, movie_ref, band_ref, edge_ref, products_in, gram_in, traces_ref, products_ref, gram_ref, products, gram):
     z, l, quad, core = position()
-    outside = jnp.logical_or(jnp.logical_and(l == 0, z == 0), jnp.logical_and(l == 1, z == planes - 1))
-    frames = movie_ref.shape[0] * movie_ref.shape[1] * movie_ref.shape[2] * movie_ref.shape[3]
-    movie = movie_ref[...].reshape(frames, movie_ref.shape[4])
-    plane = band_ref[...].reshape(frames, 256)
-    edge = jnp.where(outside, jnp.zeros((), BF16), edge_ref[...].reshape(frames, 128))
-    whole = jnp.concatenate([plane, edge], axis=1)
+    beside = jnp.where(l == 0, z, planes - 1 - z) > 0
+    its = 1 - core
+    partial_products(beside, movie_ref.at[its], band_ref.at[its], edge_ref.at[its], products, gram)
     plane_at = pl.multiple_of((1 - l) * 128, 128)
     edge_at = pl.multiple_of(l * 256, 128)
-
-    def over_frames(left):
-        return lax.dot_general(left, whole, (((0,), (0,)), ((), ())), preferred_element_type=F32)
-
-    products = over_frames(movie)
-    products_ref[:, pl.ds(plane_at, 256)] = products[:, :256]
-    products_ref[:, pl.ds(edge_at, 128)] = products[:, 256:]
-    gram = over_frames(whole)
-    gram_ref[pl.ds(plane_at, 256), pl.ds(plane_at, 256)] = gram[:256, :256]
-    gram_ref[pl.ds(plane_at, 256), pl.ds(edge_at, 128)] = gram[:256, 256:]
-    gram_ref[pl.ds(edge_at, 128), pl.ds(plane_at, 256)] = gram[256:, :256]
-    gram_ref[pl.ds(edge_at, 128), pl.ds(edge_at, 128)] = gram[256:, 256:]
+    products_ref[:, pl.ds(plane_at, 256)] = products[:, :256] + products_in[:, :256]
+    products_ref[:, pl.ds(edge_at, 128)] = products[:, 256:] + products_in[:, 256:]
+    for at, rows in ((plane_at, slice(0, 256)), (edge_at, slice(256, 384))):
+        gram_ref[pl.ds(at, rows.stop - rows.start), pl.ds(plane_at, 256)] = gram[rows, :256] + gram_in[rows, :256]
+        gram_ref[pl.ds(at, rows.stop - rows.start), pl.ds(edge_at, 128)] = gram[rows, 256:] + gram_in[rows, 256:]
     for half in range(2):
         traces_ref[half * 64:half * 64 + 64, :] = band_ref[core, half, quad, :, pl.ds(pl.multiple_of(l * 128, 128), 128)]
 
@@ -370,16 +382,18 @@
     hbm = pl.BlockSpec(memory_space=pl.ANY)
     dma = pltpu.SemaphoreType.DMA
     chunks = voxels // CHUNK
-    movie, band, edge = pl.pallas_call(
+    gathered = pl.pallas_call(
         functools.partial(exchange_kernel, planes),
         name="exchange",
         out_shape=[
             jax.ShapeDtypeStruct((2, 2, 8, half, share), BF16),
             jax.ShapeDtypeStruct((2, 2, 8, half, 256), BF16),
             jax.ShapeDtypeStruct((2, 2, 8, half, 128), BF16),
+            jax.ShapeDtypeStruct((share, 384), F32),
+            jax.ShapeDtypeStruct((384, 384), F32),
         ],
         in_specs=[hbm, hbm, hbm, hbm],
-        out_specs=[hbm, hbm, hbm],
+        out_specs=[pl.BlockSpec(memory_space=pltpu.VMEM)] * 5,
         scratch_shapes=[
             pltpu.SMEM((counts.shape[0],), jnp.int32),
             pltpu.VMEM((voxels, 384), BF16), pltpu.VMEM((2, half, voxels), BF16), pltpu.VMEM((6, rows, 128), BF16),
@@ -404,10 +418,11 @@
             jax.ShapeDtypeStruct((share, 384), F32),
             jax.ShapeDtypeStruct((384, 384), F32),
         ],
-        in_specs=[vmem, vmem, vmem],
-        out_specs=[vmem, vmem, vmem],
+        in_specs=[vmem] * 5,
+        out_specs=[vmem] * 3,
+        scratch_shapes=[pltpu.VMEM((share, 384), F32), pltpu.VMEM((384, 384), F32)],
         compiler_params=pltpu.CompilerParams(vmem_limit_bytes=32 << 20),
-    )(movie, band, edge)
+    )(*gathered)
 
 
 def solution(mesh):

time: 54.3 us -> 43.9 us (0.81)
  the two profiles are of different devices: /device:TPU:1 before, /device:TPU:193 now
where the time goes in v3:
time: 43.9 us; the launch traced here: 43.8 us
  Pallas kernels  43.1 us (98%)
  between operations  0.64 us (1%)
    pallas_call x1, Pallas kernels, body(): pl.pallas_call(functools.partial(exchange_kernel, planes), name='exchange...  41.4 us
    pallas_call x1, Pallas kernels, body(): pl.pallas_call(functools.partial(product_kernel, planes), name='products'...  1.71 us

profile of v3, /device:TPU:193, one launch (start us, length us, event | category | flops | bytes accessed | tf_op | source)
XLA Modules:
  0.0 43.8 jit_solution(16218493176311223320)
XLA Ops:
  0.6 41.4 %exchange.1 = (bf16[2,2,8,64,256]{4,3,2,1,0:T(8,128)(2,1)S(1)}, bf16[2,2,8,64,256]{4,3,2,1,0:T(8,128)(2,1)S(1)}, bf16[2,2,8,64,128]{4,3,2,1,0:T(8,128)(2,1)S(1)}, f32[256,384]{1,0:T(8,128)S(1)}, f32[384,384]{1,0:T(8,128)S(1)}) custom-call(s32[32]{0:T(128)} %counts_hbm.1, bf16[2,64,4096]{2,1,0:T(8,128)(2,1)} %bitcast.1, bf16[4096,384]{1,0:T(8,128)(2,1)} %prints_ref.1, ...), custom_call_target="tpu_custom_call" | custom-call | tf_op jit(solution)/shard_map/exchange/pallas_call | solution.py:385
  42.1 1.7 %products.1 = (bf16[128,128]{1,0:T(8,128)(2,1)}, f32[256,384]{1,0:T(8,128)}, f32[384,384]{1,0:T(8,128)}) custom-call(bf16[2,2,8,64,256]{4,3,2,1,0:T(8,128)(2,1)S(1)} %get-tuple-element.8.movie_ref, bf16[2,2,8,64,256]{4,3,2,1,0:T(8,128)(2,1)S(1)} %get-tuple-element.9.band_ref, bf16[2,2,8,64,128]{4,3,2,1,0:T(8,128)(2,1)S(1)} %get-tuple-element.10.edge_ref, ...), custom_call_target="tpu_custom_call" | custom-call | tf_op jit(solution)/shard_map/products/pallas_call | solution.py:413

commit v4 on v3

--- a/solution.py
+++ b/solution.py
@@ -27,7 +27,7 @@
     planes,
     counts_hbm, frames_ref, prints_ref, traces_ref,
     movie_ref, band_ref, edge_ref, products_ref, gram_ref,
-    counts_ref, prints, frames, tracebuf, gacc, facc,
+    counts_ref, prints, lefts, tracebuf, sums,
     part_plane, part_edge, got_plane, got_edge,
     gram_plane, gram_edge, got_gram, mixing,
     state, final, final_edge,
@@ -57,10 +57,10 @@
     offsets = [(dy, dx) for dy in range(2) for dx in range(4)]
     ring = [(dx, dc) for dx in (1, 3, 2, 0) for dc in range(2) if (dx, dc) != (0, 0)]
     barrier = pltpu.get_barrier_semaphore()
-    near = [device(z, l, turned(quad, 0, dx), (core + dc) % 2) for dx, dc in ring]
-    near += [device(z, other, quad, core), device(z, l, across, core)]
-    near = [(always, target) for target in near]
+    near = [(always, device(z, other, quad, core))]
     near += [(there, device(plane, side, quad, core)) for there, plane in ((above, up), (below, down)) for side in range(2)]
+    near += [(always, device(z, l, across, core))]
+    near += [(always, device(z, l, turned(quad, 0, dx), (core + dc) % 2)) for dx, dc in ring]
 
     rows = prints_ref.shape[0]
     chunks = rows // CHUNK
@@ -72,7 +72,8 @@
         return (
             pltpu.make_async_copy(prints_ref.at[pl.ds(at, CHUNK), pl.ds(plane_at, 256)], prints.at[pl.ds(at, CHUNK), pl.ds(0, 256)], load_sem.at[k, 0]),
             pltpu.make_async_copy(prints_ref.at[pl.ds(at, CHUNK), pl.ds(edge_at, 128)], prints.at[pl.ds(at, CHUNK), pl.ds(256, 128)], load_sem.at[k, 1]),
-            pltpu.make_async_copy(frames_ref.at[:, :, pl.ds(at, CHUNK)], frames.at[:, :, pl.ds(at, CHUNK)], load_sem.at[k, 2]),
+            pltpu.make_async_copy(frames_ref.at[0, :, pl.ds(at, CHUNK)], lefts.at[128:192, pl.ds(at, CHUNK)], load_sem.at[k, 2]),
+            pltpu.make_async_copy(frames_ref.at[1, :, pl.ds(at, CHUNK)], lefts.at[192:256, pl.ds(at, CHUNK)], load_sem.at[k, 3]),
         )
 
     own_counts = pltpu.make_async_copy(counts_hbm, counts_ref, own_sem.at[3])
@@ -93,13 +94,19 @@
     @pl.when(jnp.logical_not(below))
     def _():
         tracebuf[0:2] = jnp.zeros((2,) + tracebuf.shape[1:], BF16)
+        for step in range(1, ITERS):
+            state[step, 0] = jnp.zeros(state.shape[2:], BF16)
 
     @pl.when(jnp.logical_not(above))
     def _():
         tracebuf[4:6] = jnp.zeros((2,) + tracebuf.shape[1:], BF16)
-
-    gacc[...] = jnp.zeros_like(gacc)
-    facc[...] = jnp.zeros_like(facc)
+        for step in range(1, ITERS):
+            state[step, 2] = jnp.zeros(state.shape[2:], BF16)
+
+    @pl.when(jnp.logical_not(beside))
+    def _():
+        edge_ref[...] = jnp.zeros_like(edge_ref)
+
     own_counts.wait()
 
     def number(tile):
@@ -115,27 +122,17 @@
     live_lanes = [(lane < n).astype(F32) for n in numbers]
     own_live = jnp.concatenate([live_lanes[2], live_lanes[3]], axis=1)
 
-    def chunk_step(k, carry):
+    def turn(k):
         for copy in loads(k):
             copy.wait()
         at = pl.multiple_of(k * CHUNK, CHUNK)
-        block = prints[pl.ds(at, CHUNK), :]
-        flipped = block.T
+        flipped = prints[pl.ds(at, CHUNK), :].T
         support = jnp.sum(flipped.astype(F32) * live_rows, axis=0, keepdims=True).astype(BF16)
-        left = jnp.concatenate(
-            [flipped[256:384], frames[0, :, pl.ds(at, CHUNK)], frames[1, :, pl.ds(at, CHUNK)],
-             jnp.broadcast_to(support, (16, CHUNK))], axis=0)
-        edge = jnp.dot(left, block[:, 256:384], preferred_element_type=F32)
-        gacc[256:384, 256:384] += edge[0:128]
-        facc[:, 256:384] += edge[128:272]
-        left = jnp.concatenate([left, flipped[0:256]], axis=0)
-        plane = jnp.dot(left, block[:, 0:256], preferred_element_type=F32)
-        gacc[256:384, 0:256] += plane[0:128]
-        facc[:, 0:256] += plane[128:272]
-        gacc[0:256, 0:256] += plane[272:528]
-        return carry
-
-    chunk_step(0, 0)
+        lefts[0:128, pl.ds(at, CHUNK)] = flipped[256:384]
+        lefts[256:272, pl.ds(at, CHUNK)] = jnp.broadcast_to(support, (16, CHUNK))
+        lefts[272:528, pl.ds(at, CHUNK)] = flipped[0:256]
+
+    turn(0)
     pl.semaphore_wait(barrier, len(near) - 4 + 2 * below.astype(jnp.int32) + 2 * above.astype(jnp.int32))
     pl.semaphore_signal(met, inc=1, device_id=device(z, l, across, core), device_id_type=MESH)
 
@@ -149,9 +146,15 @@
         given(there, copy.start)
         sent.append((there, copy))
 
-    for k, (there, plane, side, slot) in enumerate(
-            [(always, z, other, 2 + l), (above, up, 0, l), (above, up, 1, l), (below, down, 0, 4 + l), (below, down, 1, 4 + l)]):
-        send(there, to(traces_ref, tracebuf.at[slot], trace_send.at[k], trace_recv.at[slot], plane, side))
+    send(always, to(traces_ref, tracebuf.at[2 + l], trace_send.at[0], trace_recv.at[2 + l], z, other))
+    send(beside, to(traces_ref, tracebuf.at[4 - 3 * l], trace_send.at[1], trace_recv.at[4 - 3 * l], outward, other))
+
+    inward = (z + planes + 1 - 2 * l) % planes
+    half_rows = [pl.ds(pl.multiple_of(side * 64, 64), 64) for side in (l, other)]
+
+    def trace_rows(k, plane, side, slot, part):
+        return to(
+            traces_ref.at[part], tracebuf.at[slot, part], trace_send.at[k], trace_recv.at[slot], plane, side)
 
     def movie_copy(dy, dx, dc):
         q, c = turned(quad, dy, dx), (core + dc) % 2
@@ -161,17 +164,23 @@
             movie_ref.at[core, :, quad], movie_send.at[slot], movie_recv.at[slot],
             device_id=device(z, l, q, c), device_id_type=MESH)
 
-    lax.fori_loop(1, chunks, chunk_step, 0)
-
-    gacc[0:256, 256:384] = gacc[256:384, 0:256].T
-    gram = gacc[...]
+    movie_copies = [movie_copy(0, dx, dc) for dx, dc in ring]
+    for copy in movie_copies:
+        copy.start()
+    for k in range(1, chunks):
+        turn(k)
+    sums[0:272, 256:384] = jnp.dot(lefts[0:272], prints[:, 256:384], preferred_element_type=F32)
+    sums[:, 0:256] = jnp.dot(lefts[...], prints[:, 0:256], preferred_element_type=F32)
+
+    sums[272:528, 256:384] = sums[0:128, 0:256].T
+    gram = jnp.concatenate([sums[272:528, :], sums[0:128, :]], axis=0)
     high = gram.astype(BF16)
     low = (gram - high.astype(F32)).astype(BF16)
     gram_plane[l] = high[:, :256]
     gram_edge[...] = high[:, 256:]
 
     own_trace.wait()
-    for there, slot in ((below, 0), (below, 1), (above, 4), (above, 5), (always, 2 + other)):
+    for there, slot in ((always, 2 + other), (beside, 1 + 3 * l)):
         given(there, to(traces_ref, tracebuf.at[slot], trace_send.at[0], trace_recv.at[slot], z, other).wait_recv)
 
     def trace(slot, live):
@@ -180,8 +189,9 @@
     edge_live = jnp.where(l == 0, live_lanes[1], live_lanes[4])
     band = jnp.concatenate(
         [trace(2, live_lanes[2]), trace(3, live_lanes[3]), trace(1 + 3 * l, edge_live)], axis=1)
-    reach = facc[128:136, :]
-    parts = facc[0:128, :] - jnp.dot(band, high, preferred_element_type=F32) - jnp.dot(band, low, preferred_element_type=F32)
+    reach = sums[256:264, :]
+    parts = sums[128:256, :] - jnp.dot(
+        jnp.concatenate([band, band], axis=1), jnp.concatenate([high, low], axis=0), preferred_element_type=F32)
     for half in range(2):
         piece = jnp.concatenate([parts[half * 64:half * 64 + 64], reach], axis=0)
         part_plane[half] = piece[:, :256]
@@ -195,15 +205,11 @@
     send(always, to(gram_plane.at[l, own_rows], gram_plane.at[l, own_rows], gram_send.at[0], gram_recv.at[2], z, other, across))
     send(beside, to(gram_edge.at[own_rows], got_gram.at[other, own_rows], gram_send.at[2], gram_recv.at[other], outward, other, across))
     send(beside, to(gram_edge.at[own_rows], got_gram.at[other, own_rows], gram_send.at[1], gram_recv.at[other], outward, l))
-    movie_copies = [movie_copy(0, dx, dc) for dx, dc in ring]
-    for copy in movie_copies:
-        copy.start()
-
-    mine = pl.ds(pl.multiple_of(l * 64, 64), 64)
-    for s in range(6):
-        value = (tracebuf[s, mine, :].astype(F32) * live_lanes[s]).astype(BF16)
-        state[0, s // 2, :, (s % 2) * 128:(s % 2) * 128 + 128] = value
-
+
+
+    send(above, trace_rows(2, up, l, l, half_rows[0]))
+    send(below, trace_rows(3, down, l, 4 + l, half_rows[0]))
+    send(jnp.where(l == 0, z < planes - 1, z > 0), trace_rows(4, inward, other, 5 * l, half_rows[1]))
     to(part_plane.at[0], got_plane, part_send.at[0], part_recv.at[2], z, other).wait_recv()
     for there, slot in ((below, 0), (above, 1)):
         given(there, to(part_edge.at[0], got_edge.at[slot], part_send.at[0], part_recv.at[slot], z, other).wait_recv)
@@ -220,13 +226,25 @@
         send(above, to(state.at[step, 1], state.at[step, 0], state_send.at[step, 0], state_recv.at[step, 0], up, l))
         send(below, to(state.at[step, 1], state.at[step, 2], state_send.at[step, 1], state_recv.at[step, 1], down, l))
 
+    mine = half_rows[0]
+
+    def start_state(slots):
+        for s in slots:
+            value = (tracebuf[s, mine, :].astype(F32) * live_lanes[s]).astype(BF16)
+            state[0, s // 2, :, (s % 2) * 128:(s % 2) * 128 + 128] = value
+
+    start_state((2, 3))
     state[1, 1] = updated(state[0, 1], slope)
     send_state(1)
 
-    late_movie = [movie_copy(1, dx, dc) for dx in (0, 2, 1, 3) for dc in range(2)]
+    late_movie = [movie_copy(1, dx, dc) for dc in range(2) for dx in (2, 1, 3, 0)]
     for copy in late_movie:
         copy.start()
     movie_copies += late_movie
+
+    for there, slot in ((below, l), (above, 4 + l), (jnp.where(l == 0, z < planes - 1, z > 0), 5 - 5 * l)):
+        given(there, trace_rows(2, z, other, slot, half_rows[0]).wait_recv)
+    start_state((0, 1, 4, 5))
 
     sibling = (z * 2 + l, quad * 2 + 1 - core)
 
@@ -263,21 +281,24 @@
     mixing[640:768, 0:128] = jnp.zeros((128, 128), BF16)
     mixing[640:768, 128:256] = gd[128:256].astype(BF16)
 
-    def mixed_own(step):
-        return jnp.dot(state[step, 1], mixing[256:512], preferred_element_type=F32)
-
-    def mixed_next(step):
-        left = jnp.where(below, state[step, 0], jnp.zeros((), BF16))
-        right = jnp.where(above, state[step, 2], jnp.zeros((), BF16))
-        return (jnp.dot(left, mixing[0:256], preferred_element_type=F32)
-                + jnp.dot(right, mixing[512:768], preferred_element_type=F32))
-
-    base = slope + mixed_own(0) + mixed_next(0)
-    for step in range(1, ITERS):
-        partial = base - mixed_own(step)
+    def arrived(step):
         for there, side, slot in ((below, 0, 0), (above, 1, 2)):
             given(there, to(state.at[step, 1], state.at[step, slot], state_send.at[step, side], state_recv.at[step, side], z, other).wait_recv)
-        value = updated(state[step, 1], partial - mixed_next(step))
+
+    base = slope
+    for step in range(1, ITERS):
+        first = 0 if step == 1 else step
+        own = jnp.dot(
+            jnp.concatenate([state[k, 1] for k in range(first, step + 1)], axis=0), mixing[256:512], preferred_element_type=F32)
+        arrived(step)
+        mix = own
+        for slot in (0, 2):
+            sides = jnp.concatenate([state[k, slot] for k in range(first, step + 1)], axis=0)
+            mix = mix + jnp.dot(sides, mixing[slot * 256:slot * 256 + 256], preferred_element_type=F32)
+        if step == 1:
+            base = base + mix[:64]
+            mix = mix[64:]
+        value = updated(state[step, 1], base - mix)
         if step < ITERS - 1:
             state[step + 1, 1] = value
             send_state(step + 1)
@@ -300,7 +321,7 @@
 
     own_band = pltpu.make_async_copy(final, band_ref.at[core, l, quad], own_sem.at[2])
     own_band.start()
-    batches = [("edge", 1, 0), ("band", 1, 0), ("edge", 1, 1), ("band", 0, 1), ("edge", 0, 0), ("band", 1, 1), ("edge", 0, 1), ("band", 0, 0)]
+    batches = [("edge", 1, 0), ("edge", 1, 1), ("band", 1, 0), ("band", 1, 1), ("edge", 0, 0), ("edge", 0, 1), ("band", 0, 1), ("band", 0, 0)]
     for kind, dy, side in batches:
         for dx in (2, 1, 3, 0):
             if kind == "edge":
@@ -314,9 +335,6 @@
             return edge_ref.at[c, side, pl.ds(yh * 4, 4)]
         return band_ref.at[c, (l + side) % 2, pl.ds(yh * 4, 4)]
 
-    own_movie.wait()
-    for copy in movie_copies:
-        copy.wait_recv()
     for k, (kind, dy, side) in enumerate(batches):
         there = beside if kind == "edge" else always
         for dx in range(4):
@@ -333,37 +351,49 @@
         send(there, pltpu.make_async_remote_copy(
             ref, ref, pass_send.at[3 + k], pass_recv.at[3 + k], device_id=sibling, device_id_type=MESH))
 
-    partial_products(beside, movie_ref.at[core], band_ref.at[core], edge_ref.at[core], products_ref, gram_ref)
-
+    def passed(k):
+        kind, dy, side = batches[k]
+        ref = row_of(kind, dy, side, 1 - core)
+        given(beside if kind == "edge" else always, pltpu.make_async_remote_copy(
+            ref, ref, pass_send.at[3 + k], pass_recv.at[3 + k], device_id=sibling, device_id_type=MESH).wait_recv)
+
+    own_movie.wait()
+    for copy in movie_copies:
+        copy.wait_recv()
+    every = slice(None)
+    products_ref[...], gram_ref[...] = partial_products(core, every, movie_ref, band_ref, edge_ref)
+    for k in range(4):
+        passed(k)
+    products, gram = partial_products(1 - core, row_slice(across), movie_ref, band_ref, edge_ref)
+    products_ref[...] += products
+    gram_ref[...] += gram
+    for k in range(4, 8):
+        passed(k)
     for there, copy in sent:
         given(there, copy.wait_send)
     for copy in movie_copies:
         copy.wait_send()
-    for k, (kind, dy, side) in enumerate(batches):
-        ref = row_of(kind, dy, side, 1 - core)
-        given(beside if kind == "edge" else always, pltpu.make_async_remote_copy(
-            ref, ref, pass_send.at[3 + k], pass_recv.at[3 + k], device_id=sibling, device_id_type=MESH).wait_recv)
-
-
-def partial_products(beside, movie_ref, band_ref, edge_ref, products_ref, gram_ref):
-    frames = movie_ref.shape[0] * movie_ref.shape[1] * movie_ref.shape[2]
-    movie = movie_ref[...].reshape(frames, movie_ref.shape[3])
-    plane = band_ref[...].reshape(frames, 256)
-    edge = jnp.where(beside, edge_ref[...].reshape(frames, 128), jnp.zeros((), BF16))
-    whole = jnp.concatenate([plane, edge], axis=1)
+
+
+def row_slice(quad):
+    return pl.ds(quad // 4 * 4, 4)
+
+
+def partial_products(core, row, movie_ref, band_ref, edge_ref):
+    def frames_of(ref):
+        return ref[core, :, row].reshape(-1, ref.shape[-1])
+
+    whole = jnp.concatenate([frames_of(band_ref), frames_of(edge_ref)], axis=1)
 
     def over_frames(left):
         return lax.dot_general(left, whole, (((0,), (0,)), ((), ())), preferred_element_type=F32)
 
-    products_ref[...] = over_frames(movie)
-    gram_ref[...] = over_frames(whole)
-
-
-def product_kernel(planes, movie_ref, band_ref, edge_ref, products_in, gram_in, traces_ref, products_ref, gram_ref, products, gram):
+    return over_frames(frames_of(movie_ref)), over_frames(whole)
+
+
+def product_kernel(movie_ref, band_ref, edge_ref, products_in, gram_in, traces_ref, products_ref, gram_ref):
     z, l, quad, core = position()
-    beside = jnp.where(l == 0, z, planes - 1 - z) > 0
-    its = 1 - core
-    partial_products(beside, movie_ref.at[its], band_ref.at[its], edge_ref.at[its], products, gram)
+    products, gram = partial_products(1 - core, row_slice(quad), movie_ref, band_ref, edge_ref)
     plane_at = pl.multiple_of((1 - l) * 128, 128)
     edge_at = pl.multiple_of(l * 256, 128)
     products_ref[:, pl.ds(plane_at, 256)] = products[:, :256] + products_in[:, :256]
@@ -396,14 +426,14 @@
         out_specs=[pl.BlockSpec(memory_space=pltpu.VMEM)] * 5,
         scratch_shapes=[
             pltpu.SMEM((counts.shape[0],), jnp.int32),
-            pltpu.VMEM((voxels, 384), BF16), pltpu.VMEM((2, half, voxels), BF16), pltpu.VMEM((6, rows, 128), BF16),
-            pltpu.VMEM((384, 384), F32), pltpu.VMEM((rows + 16, 384), F32),
+            pltpu.VMEM((voxels, 384), BF16), pltpu.VMEM((400 + rows, voxels), BF16), pltpu.VMEM((6, rows, 128), BF16),
+            pltpu.VMEM((400 + rows, 384), F32),
             pltpu.VMEM((2, half + 8, 256), F32), pltpu.VMEM((2, half + 8, 128), F32),
             pltpu.VMEM((half + 8, 256), F32), pltpu.VMEM((2, half + 8, 128), F32),
             pltpu.VMEM((2, 384, 256), BF16), pltpu.VMEM((384, 128), BF16), pltpu.VMEM((2, 384, 128), BF16),
             pltpu.VMEM((768, 256), BF16),
             pltpu.VMEM((ITERS, 3, half, 256), BF16), pltpu.VMEM((half, 256), BF16), pltpu.VMEM((2, half, 128), BF16),
-            dma((chunks, 3)), dma((16,)), dma((16,)), dma((5,)), dma((6,)), dma((3,)), dma((3,)),
+            dma((chunks, 4)), dma((16,)), dma((16,)), dma((5,)), dma((6,)), dma((3,)), dma((3,)),
             dma((3,)), dma((3,)), dma((ITERS, 2)), dma((ITERS, 2)), dma((16,)), dma((16,)),
             dma((2, 8)), dma((2, 8)), dma((11,)), dma((11,)), dma((4,)), pltpu.SemaphoreType.REGULAR,
         ],
@@ -411,7 +441,7 @@
     )(*[pltpu.with_memory_space_constraint(v, pltpu.HBM) for v in (counts, frames_data.reshape(2, half, voxels), footprints, traces)])
     vmem = pl.BlockSpec(memory_space=pltpu.VMEM)
     return pl.pallas_call(
-        functools.partial(product_kernel, planes),
+        product_kernel,
         name="products",
         out_shape=[
             jax.ShapeDtypeStruct((rows, 128), BF16),
@@ -420,7 +450,6 @@
         ],
         in_specs=[vmem] * 5,
         out_specs=[vmem] * 3,
-        scratch_shapes=[pltpu.VMEM((share, 384), F32), pltpu.VMEM((384, 384), F32)],
         compiler_params=pltpu.CompilerParams(vmem_limit_bytes=32 << 20),
     )(*gathered)
 

time: 43.9 us -> 48.1 us (1.096)
  the two profiles are of different devices: /device:TPU:193 before, /device:TPU:177 now
where the time goes in v4:
time: 48.1 us; the launch traced here: 48 us
  Pallas kernels  47.4 us (99%)
  between operations  0.64 us (1%)
    pallas_call x1, Pallas kernels, body(): pl.pallas_call(functools.partial(exchange_kernel, planes), name='exchange...  46 us
    pallas_call x1, Pallas kernels, body(): pl.pallas_call(product_kernel, name='products', out_shape=[jax.ShapeDtype...  1.39 us

profile of v4, /device:TPU:177, one launch (start us, length us, event | category | flops | bytes accessed | tf_op | source)
XLA Modules:
  0.0 48.0 jit_solution(9088975887183776849)
XLA Ops:
  0.6 46.0 %exchange.1 = (bf16[2,2,8,64,256]{4,3,2,1,0:T(8,128)(2,1)S(1)}, bf16[2,2,8,64,256]{4,3,2,1,0:T(8,128)(2,1)S(1)}, bf16[2,2,8,64,128]{4,3,2,1,0:T(8,128)(2,1)S(1)}, f32[256,384]{1,0:T(8,128)S(1)}, f32[384,384]{1,0:T(8,128)S(1)}) custom-call(s32[32]{0:T(128)} %counts_hbm.1, bf16[2,64,4096]{2,1,0:T(8,128)(2,1)} %bitcast.1, bf16[4096,384]{1,0:T(8,128)(2,1)} %prints_ref.1, ...), custom_call_target="tpu_custom_call" | custom-call | tf_op jit(solution)/shard_map/exchange/pallas_call | solution.py:415
  46.6 1.4 %products.1 = (bf16[128,128]{1,0:T(8,128)(2,1)}, f32[256,384]{1,0:T(8,128)}, f32[384,384]{1,0:T(8,128)}) custom-call(bf16[2,2,8,64,256]{4,3,2,1,0:T(8,128)(2,1)S(1)} %get-tuple-element.8.movie_ref, bf16[2,2,8,64,256]{4,3,2,1,0:T(8,128)(2,1)S(1)} %get-tuple-element.9.band_ref, bf16[2,2,8,64,128]{4,3,2,1,0:T(8,128)(2,1)S(1)} %get-tuple-element.10.edge_ref, ...), custom_call_target="tpu_custom_call" | custom-call | tf_op jit(solution)/shard_map/products/pallas_call | solution.py:443

commit v5 on v4

--- a/solution.py
+++ b/solution.py
@@ -164,9 +164,6 @@
             movie_ref.at[core, :, quad], movie_send.at[slot], movie_recv.at[slot],
             device_id=device(z, l, q, c), device_id_type=MESH)
 
-    movie_copies = [movie_copy(0, dx, dc) for dx, dc in ring]
-    for copy in movie_copies:
-        copy.start()
     for k in range(1, chunks):
         turn(k)
     sums[0:272, 256:384] = jnp.dot(lefts[0:272], prints[:, 256:384], preferred_element_type=F32)
@@ -205,7 +202,9 @@
     send(always, to(gram_plane.at[l, own_rows], gram_plane.at[l, own_rows], gram_send.at[0], gram_recv.at[2], z, other, across))
     send(beside, to(gram_edge.at[own_rows], got_gram.at[other, own_rows], gram_send.at[2], gram_recv.at[other], outward, other, across))
     send(beside, to(gram_edge.at[own_rows], got_gram.at[other, own_rows], gram_send.at[1], gram_recv.at[other], outward, l))
-
+    movie_copies = [movie_copy(0, dx, dc) for dx, dc in ring]
+    for copy in movie_copies:
+        copy.start()
 
     send(above, trace_rows(2, up, l, l, half_rows[0]))
     send(below, trace_rows(3, down, l, 4 + l, half_rows[0]))

time: 48.1 us -> 43.4 us (0.902)
  the two profiles are of different devices: /device:TPU:177 before, /device:TPU:225 now
where the time goes in v5:
time: 43.4 us; the launch traced here: 43.3 us
  Pallas kernels  42.7 us (98%)
  between operations  0.64 us (1%)
    pallas_call x1, Pallas kernels, body(): pl.pallas_call(functools.partial(exchange_kernel, planes), name='exchange...  41.3 us
    pallas_call x1, Pallas kernels, body(): pl.pallas_call(product_kernel, name='products', out_shape=[jax.ShapeDtype...  1.39 us

profile of v5, /device:TPU:225, one launch (start us, length us, event | category | flops | bytes accessed | tf_op | source)
XLA Modules:
  0.0 43.3 jit_solution(16794734211969988408)
XLA Ops:
  0.6 41.3 %exchange.1 = (bf16[2,2,8,64,256]{4,3,2,1,0:T(8,128)(2,1)S(1)}, bf16[2,2,8,64,256]{4,3,2,1,0:T(8,128)(2,1)S(1)}, bf16[2,2,8,64,128]{4,3,2,1,0:T(8,128)(2,1)S(1)}, f32[256,384]{1,0:T(8,128)S(1)}, f32[384,384]{1,0:T(8,128)S(1)}) custom-call(s32[32]{0:T(128)} %counts_hbm.1, bf16[2,64,4096]{2,1,0:T(8,128)(2,1)} %bitcast.1, bf16[4096,384]{1,0:T(8,128)(2,1)} %prints_ref.1, ...), custom_call_target="tpu_custom_call" | custom-call | tf_op jit(solution)/shard_map/exchange/pallas_call | solution.py:414
  41.9 1.4 %products.1 = (bf16[128,128]{1,0:T(8,128)(2,1)}, f32[256,384]{1,0:T(8,128)}, f32[384,384]{1,0:T(8,128)}) custom-call(bf16[2,2,8,64,256]{4,3,2,1,0:T(8,128)(2,1)S(1)} %get-tuple-element.8.movie_ref, bf16[2,2,8,64,256]{4,3,2,1,0:T(8,128)(2,1)S(1)} %get-tuple-element.9.band_ref, bf16[2,2,8,64,128]{4,3,2,1,0:T(8,128)(2,1)S(1)} %get-tuple-element.10.edge_ref, ...), custom_call_target="tpu_custom_call" | custom-call | tf_op jit(solution)/shard_map/products/pallas_call | solution.py:442

commit v6 on v5

--- a/solution.py
+++ b/solution.py
@@ -176,6 +176,12 @@
     gram_plane[l] = high[:, :256]
     gram_edge[...] = high[:, 256:]
 
+    pl.semaphore_wait(met, 1)
+    own_rows = pl.ds(pl.multiple_of(core * 192, 64), 192)
+    send(always, to(gram_plane.at[l, own_rows], gram_plane.at[l, own_rows], gram_send.at[0], gram_recv.at[2], z, other, across))
+    send(beside, to(gram_edge.at[own_rows], got_gram.at[other, own_rows], gram_send.at[2], gram_recv.at[other], outward, other, across))
+    send(beside, to(gram_edge.at[own_rows], got_gram.at[other, own_rows], gram_send.at[1], gram_recv.at[other], outward, l))
+
     own_trace.wait()
     for there, slot in ((always, 2 + other), (beside, 1 + 3 * l)):
         given(there, to(traces_ref, tracebuf.at[slot], trace_send.at[0], trace_recv.at[slot], z, other).wait_recv)
@@ -193,15 +199,10 @@
         piece = jnp.concatenate([parts[half * 64:half * 64 + 64], reach], axis=0)
         part_plane[half] = piece[:, :256]
         part_edge[half] = piece[:, 256:]
-    pl.semaphore_wait(met, 1)
 
     send(always, to(part_plane.at[other], got_plane, part_send.at[0], part_recv.at[2], z, other))
     send(beside, to(part_edge.at[other], got_edge.at[other], part_send.at[2], part_recv.at[other], outward, other))
     send(beside, to(part_edge.at[l], got_edge.at[other], part_send.at[1], part_recv.at[other], outward, l))
-    own_rows = pl.ds(pl.multiple_of(core * 192, 64), 192)
-    send(always, to(gram_plane.at[l, own_rows], gram_plane.at[l, own_rows], gram_send.at[0], gram_recv.at[2], z, other, across))
-    send(beside, to(gram_edge.at[own_rows], got_gram.at[other, own_rows], gram_send.at[2], gram_recv.at[other], outward, other, across))
-    send(beside, to(gram_edge.at[own_rows], got_gram.at[other, own_rows], gram_send.at[1], gram_recv.at[other], outward, l))
     movie_copies = [movie_copy(0, dx, dc) for dx, dc in ring]
     for copy in movie_copies:
         copy.start()

time: 43.4 us -> 45.2 us (1.041)
  the two profiles are of different devices: /device:TPU:225 before, /device:TPU:97 now
where the time goes in v6:
time: 45.2 us; the launch traced here: 45.1 us
  Pallas kernels  44.4 us (98%)
  between operations  0.64 us (1%)
    pallas_call x1, Pallas kernels, body(): pl.pallas_call(functools.partial(exchange_kernel, planes), name='exchange...  43 us
    pallas_call x1, Pallas kernels, body(): pl.pallas_call(product_kernel, name='products', out_shape=[jax.ShapeDtype...  1.39 us

profile of v6, /device:TPU:97, one launch (start us, length us, event | category | flops | bytes accessed | tf_op | source)
XLA Modules:
  0.0 45.1 jit_solution(1574518433121256068)
XLA Ops:
  0.6 43.0 %exchange.1 = (bf16[2,2,8,64,256]{4,3,2,1,0:T(8,128)(2,1)S(1)}, bf16[2,2,8,64,256]{4,3,2,1,0:T(8,128)(2,1)S(1)}, bf16[2,2,8,64,128]{4,3,2,1,0:T(8,128)(2,1)S(1)}, f32[256,384]{1,0:T(8,128)S(1)}, f32[384,384]{1,0:T(8,128)S(1)}) custom-call(s32[32]{0:T(128)} %counts_hbm.1, bf16[2,64,4096]{2,1,0:T(8,128)(2,1)} %bitcast.1, bf16[4096,384]{1,0:T(8,128)(2,1)} %prints_ref.1, ...), custom_call_target="tpu_custom_call" | custom-call | tf_op jit(solution)/shard_map/exchange/pallas_call | solution.py:415
  43.7 1.4 %products.1 = (bf16[128,128]{1,0:T(8,128)(2,1)}, f32[256,384]{1,0:T(8,128)}, f32[384,384]{1,0:T(8,128)}) custom-call(bf16[2,2,8,64,256]{4,3,2,1,0:T(8,128)(2,1)S(1)} %get-tuple-element.8.movie_ref, bf16[2,2,8,64,256]{4,3,2,1,0:T(8,128)(2,1)S(1)} %get-tuple-element.9.band_ref, bf16[2,2,8,64,128]{4,3,2,1,0:T(8,128)(2,1)S(1)} %get-tuple-element.10.edge_ref, ...), custom_call_target="tpu_custom_call" | custom-call | tf_op jit(solution)/shard_map/products/pallas_call | solution.py:443
